TPU v7x, 256 devices: a whole 4x4x8 slice. The times are simulated.
256 devices in a mesh: dp: 2 (over core), block: 128 (over z, y, x).
Axes of the slice: x: 4, y: 4, z: 8, core: 2. Of those that a mesh axis runs over, the one named last changes fastest.
Arguments:
- features: bfloat16 [2, 128, 16, 16, 8, 128], P('dp', 'block'), may hold values from -6 to 6
- mask_margin: int32 [2, 128, 18, 18, 10], P('dp', 'block'), may hold values from 0 to 1, as said below
- brick_list: int32 [2, 128, 4], P('dp', 'block'), may hold values from 0 to 8, as said below
- kernel_weight: bfloat16 [27, 128, 128], replicated, may hold values from -0.109375 to 0.109375
- cotangent: bfloat16 [2, 128, 16, 16, 8, 128], P('dp', 'block'), may hold values from -6 to 6
Outputs:
- output: bfloat16 [2, 128, 16, 16, 8, 128], P('dp', 'block')
- input_grad: bfloat16 [2, 128, 16, 16, 8, 128], P('dp', 'block')
- weight_grad: float32 [442368], P('block')
Inputs may be any that keep to these rules, and one draw needn't show every extreme that they name: `brick_list`: for each tile and block the leading entries are distinct local brick indices, at least one and at most 4 of them; the remaining entries equal 8; in every tile some block lists exactly 4 bricks. `mask_margin`: A margin entry equals the neighbouring block's entry for the same cell if that cell's brick is listed by the neighbouring block, and 0 otherwise; cells outside the tile are 0.
All inputs are finite; a program needn't handle non-finite values.
Results may differ from a plain program's by a relative error of at most 0.001.
Values may be sent and summed in bfloat16 or wider, within the bound.
A program may use at most 128 MiB of HBM per device.

v0:
```python
import math

import jax
import jax.numpy as jnp
from jax import lax
from jax.sharding import PartitionSpec as P

BRICK_X = 8
BRICK_Y = 8
BRICK_Z = 4
GRID_Y = 8
BX_DEV = 2
BY_DEV = 2
BZ_DEV = 2
LX = 16
LY = 16
LZ = 8
NB_DEV = 8


def passed_along(value, axis, steps):
    count = lax.axis_size(axis)
    first, last = (max(0, -steps), min(count, count - steps))
    return lax.ppermute(value, axis, [(source, source + steps) for source in range(first, last)])


def listed_cells(listing):
    brick_ids = jnp.arange(NB_DEV, dtype=jnp.int32)
    listed = jnp.any(brick_ids[:, None] == listing[None, :], axis=1).astype(jnp.int32)
    shaped = listed.reshape(BX_DEV, 1, BY_DEV, 1, BZ_DEV, 1)
    spread_out = jnp.broadcast_to(shaped, (BX_DEV, BRICK_X, BY_DEV, BRICK_Y, BZ_DEV, BRICK_Z))
    return spread_out.reshape(LX, LY, LZ)


def with_margin(local_field):
    column = lax.axis_index("block") % GRID_Y
    extent_x = local_field.shape[0]
    extent_y = local_field.shape[1]
    row_faces = []
    for toward in (1, -1):
        border = local_field[extent_x - 1 : extent_x] if toward == 1 else local_field[0:1]
        row_faces.append(passed_along(border, "block", toward * GRID_Y))
    column_faces = []
    for toward in (1, -1):
        border = local_field[:, extent_y - 1 : extent_y] if toward == 1 else local_field[:, 0:1]
        arrived = passed_along(border, "block", toward)
        accept = column != 0 if toward == 1 else column != GRID_Y - 1
        column_faces.append(jnp.where(accept, arrived, jnp.zeros_like(arrived)))
    corners = {}
    for toward_x in (1, -1):
        for toward_y in (1, -1):
            row_at = extent_x - 1 if toward_x == 1 else 0
            col_at = extent_y - 1 if toward_y == 1 else 0
            corner_piece = local_field[row_at : row_at + 1, col_at : col_at + 1]
            arrived = passed_along(corner_piece, "block", toward_x * GRID_Y + toward_y)
            accept = column != 0 if toward_y == 1 else column != GRID_Y - 1
            corners[toward_x, toward_y] = jnp.where(accept, arrived, jnp.zeros_like(arrived))
    top_band = jnp.concatenate([corners[1, 1], row_faces[0], corners[1, -1]], axis=1)
    middle_band = jnp.concatenate([column_faces[0], local_field, column_faces[1]], axis=1)
    bottom_band = jnp.concatenate([corners[-1, 1], row_faces[1], corners[-1, -1]], axis=1)
    extended = jnp.concatenate([top_band, middle_band, bottom_band], axis=0)
    return jnp.pad(extended, ((0, 0), (0, 0), (1, 1), (0, 0)))


def convolve(feat_full, grad_full, forward_w, backward_w):
    extent_x = feat_full.shape[-4] - 2
    extent_y = feat_full.shape[-3] - 2
    extent_z = feat_full.shape[-2] - 2
    channels = feat_full.shape[-1]
    inside_grad = grad_full[..., 1:-1, 1:-1, 1:-1, :].reshape(-1, channels)
    forward_acc = jnp.zeros((inside_grad.shape[0], channels), jnp.float32)
    backward_acc = jnp.zeros((inside_grad.shape[0], channels), jnp.float32)
    weight_rows = []
    for shift_x in range(3):
        for shift_y in range(3):
            group_index = 3 * shift_x + shift_y
            feat_stack = jnp.concatenate(
                [
                    feat_full[
                        ...,
                        shift_x : shift_x + extent_x,
                        shift_y : shift_y + extent_y,
                        shift_z : shift_z + extent_z,
                        :,
                    ]
                    for shift_z in range(3)
                ],
                axis=-1,
            ).reshape(-1, 3 * channels)
            grad_stack = jnp.concatenate(
                [
                    grad_full[
                        ...,
                        2 - shift_x : 2 - shift_x + extent_x,
                        2 - shift_y : 2 - shift_y + extent_y,
                        2 - shift_z : 2 - shift_z + extent_z,
                        :,
                    ]
                    for shift_z in range(3)
                ],
                axis=-1,
            ).reshape(-1, 3 * channels)
            forward_acc = forward_acc + jnp.dot(
                feat_stack, forward_w[group_index], preferred_element_type=jnp.float32
            )
            backward_acc = backward_acc + jnp.dot(
                grad_stack, backward_w[group_index], preferred_element_type=jnp.float32
            )
            weight_rows.append(
                lax.dot_general(
                    feat_stack,
                    inside_grad,
                    (((0,), (0,)), ((), ())),
                    preferred_element_type=jnp.float32,
                )
            )
    return (forward_acc, backward_acc, jnp.stack(weight_rows))


def body(features, mask_margin, brick_list, kernel_weight, cotangent):
    local_field = features[0, 0]
    local_grad = cotangent[0, 0]
    margin = mask_margin[0, 0]
    listing = brick_list[0, 0]
    channels = local_field.shape[-1]
    active = margin * jnp.pad(listed_cells(listing), 1, constant_values=1)
    active_cells = active.astype(jnp.bfloat16)[..., None]
    feat_full = with_margin(local_field) * active_cells
    grad_full = with_margin(local_grad) * active_cells
    inside = active[1:-1, 1:-1, 1:-1].astype(jnp.float32)[..., None]
    forward_w = kernel_weight.reshape(9, 3 * channels, channels)
    backward_w = jnp.swapaxes(kernel_weight, 1, 2).reshape(9, 3 * channels, channels)
    forward_acc, backward_acc, weight_acc = convolve(feat_full, grad_full, forward_w, backward_w)
    forward_grid = forward_acc.reshape(LX, LY, LZ, channels)
    backward_grid = backward_acc.reshape(LX, LY, LZ, channels)
    output = (forward_grid * inside).astype(jnp.bfloat16)
    input_grad = (backward_grid * inside).astype(jnp.bfloat16)
    weight_flat = weight_acc.reshape(-1)
    scale_factor = 1.0 / math.sqrt(lax.axis_size("dp") * lax.axis_size("block") * LX * LY * LZ)
    summed = lax.psum(weight_flat, ("dp", "block"))
    share_len = weight_flat.shape[0] // lax.axis_size("block")
    own_share = lax.dynamic_slice_in_dim(summed, lax.axis_index("block") * share_len, share_len)
    return (output[None, None], input_grad[None, None], own_share * scale_factor)


def solution(mesh):
    return jax.shard_map(
        body,
        mesh=mesh,
        in_specs=(
            P("dp", "block", None, None, None, None),
            P("dp", "block", None, None, None),
            P("dp", "block", None),
            P(),
            P("dp", "block", None, None, None, None),
        ),
        out_specs=(
            P("dp", "block", None, None, None, None),
            P("dp", "block", None, None, None, None),
            P("block"),
        ),
        check_vma=False,
    )
```

profile of v0, /device:TPU:1, one launch (start us, length us, event | category | flops | bytes accessed | tf_op | source)
XLA Modules:
  0.0 392.7 jit_solution(14346985935776887495)
XLA Ops:
  7.2 1.2 copy.90
  8.4 0.6 fusion.37
  9.1 1.3 collective-permute-start.5
  10.3 8.2 %collective-permute-start = (bf16[1,1,8,128]{3,1,2,0:T(2,128)(2,1)}, bf16[1,1,8,128]{3,1,2,0:T(2,128)(2,1)S(1)}, u32[]{:S(2)}, u32[]{:S(2)}) collective-permute-start(bf16[1,1,8,128]{3,1,2,0:T(2,128)(2,1)} %get-tuple-element.87), channel_id=1, source_target_pairs={{0,9},{1,10},{2,11},{3,12},{4,13},{5,14},{6,15},{7,16},{8,17},{9,1... | collective-permute-start | bytes 6152 | tf_op jit(solution)/shard_map/ppermute | solution.py:24
  18.5 1.1 copy.89
  19.7 0.6 fusion.34
  20.3 5.4 %collective-permute-start.10 = (bf16[1,1,8,128]{3,1,2,0:T(2,128)(2,1)}, bf16[1,1,8,128]{3,1,2,0:T(2,128)(2,1)S(1)}, u32[]{:S(2)}, u32[]{:S(2)}) collective-permute-start(bf16[1,1,8,128]{3,1,2,0:T(2,128)(2,1)} %get-tuple-element.80), channel_id=1, source_target_pairs={{0,7},{1,8},{2,9},{3,10},{4,11},{5,12},{6,13},{7,14},{8,15},{9,16}... | collective-permute-start | bytes 6152 | tf_op jit(solution)/shard_map/ppermute | solution.py:24
  25.7 1.3 collective-permute-start.7
  27.0 2.4 collective-permute-start.2
  29.4 0.8 fusion.35
  30.1 0.7 fusion.38
  30.9 0.6 slice_bitcast_fusion.3
  31.5 1.0 fusion.33
  32.5 1.3 copy.65
  34.4 0.9 fusion.32
  35.7 1.3 collective-permute-start.13
  37.0 11.1 %collective-permute-start.8 = (bf16[1,1,8,128]{3,1,2,0:T(2,128)(2,1)S(1)}, bf16[1,1,8,128]{3,1,2,0:T(2,128)(2,1)S(1)}, u32[]{:S(2)}, u32[]{:S(2)}) collective-permute-start(bf16[1,1,8,128]{3,1,2,0:T(2,128)(2,1)S(1)} %copy-done.58), channel_id=1, source_target_pairs={{0,9},{1,10},{2,11},{3,12},{4,13},{5,14},{6,15},{7,16},{8,17},{9,1... | collective-permute-start | bytes 6152 | tf_op jit(solution)/shard_map/ppermute | solution.py:24
  48.1 1.3 collective-permute-start.15
  49.5 1.3 collective-permute-start.12
  50.8 1.3 collective-permute-start.4
  52.1 4.7 %collective-permute-start.11 = (bf16[16,1,8,128]{3,1,2,0:T(2,128)(2,1)S(1)}, bf16[16,1,8,128]{3,1,2,0:T(2,128)(2,1)S(1)}, u32[]{:S(2)}, u32[]{:S(2)}) collective-permute-start(bf16[16,1,8,128]{3,1,2,0:T(2,128)(2,1)S(1)} %copy-done.52), channel_id=1, source_target_pairs={{0,1},{1,2},{2,3},{3,4},{4,5},{5,6},{6,7},{7,8},{8,9},{9,10},{10,1... | collective-permute-start | bytes 98312 | tf_op jit(solution)/shard_map/ppermute | solution.py:24
  56.8 3.4 collective-permute-start.3
  60.3 5.2 %collective-permute-start.1 = (bf16[1,16,8,128]{3,1,2,0:T(8,128)(2,1)S(1)}, bf16[1,16,8,128]{3,1,2,0:T(8,128)(2,1)S(1)}, u32[]{:S(2)}, u32[]{:S(2)}) collective-permute-start(bf16[1,16,8,128]{3,1,2,0:T(8,128)(2,1)S(1)} %copy-done.56), channel_id=1, source_target_pairs={{0,8},{1,9},{2,10},{3,11},{4,12},{5,13},{6,14},{7,15},{8,16},{9,17... | collective-permute-start | bytes 98312 | tf_op jit(solution)/shard_map/ppermute | solution.py:24
  65.5 1.3 collective-permute-start.14
  66.9 1.3 collective-permute-start.6
  68.3 7.8 %collective-permute-start.9 = (bf16[1,16,8,128]{3,1,2,0:T(8,128)(2,1)S(1)}, bf16[1,16,8,128]{3,1,2,0:T(8,128)(2,1)S(1)}, u32[]{:S(2)}, u32[]{:S(2)}) collective-permute-start(bf16[1,16,8,128]{3,1,2,0:T(8,128)(2,1)S(1)} %get-tuple-element.81), channel_id=1, source_target_pairs={{0,8},{1,9},{2,10},{3,11},{4,12},{5,13},{6,14},{7,15},{8,16},{9,17... | collective-permute-start | bytes 98312 | tf_op jit(solution)/shard_map/ppermute | solution.py:24
  76.3 0.8 collective-permute-done.9
  77.1 4.4 %fusion.11 = (bf16[18,18,10,128]{3,1,2,0:T(8,128)(2,1)S(1)}, bf16[18,18,10,128]{3,1,2,0:T(8,128)(2,1)S(1)}) fusion(bf16[1,1,8,128]{3,1,2,0:T(2,128)(2,1)S(1)} %broadcast_select_fusion.4, bf16[1,16,8,128]{3,1,2,0:T(8,128)(2,1)S(1)} %collective-permute-done.14, bf16[1,1,8,128]{3,1,2,0:T(2,128)(2,1)S(1)} %broadcast_select_fusion.8, ...), kind=kLoop, calls=%fused_computation.57 | loop fusion | flops 24883200 | bytes 2992464 | tf_op jit(solution)/shard_map/mul | solution.py:129
  81.5 0.9 fusion.31
  82.5 2.6 fusion.30
  85.0 4.2 %fusion.28 = (bf16[16,16,8,128]{3,1,2,0:T(8,128)(2,1)}, bf16[16,16,8,128]{3,1,2,0:T(8,128)(2,1)}, bf16[16,16,8,128]{3,1,2,0:T(8,128)(2,1)}, bf16[16,16,8,128]{3,...) fusion(bf16[18,18,10,128]{3,1,2,0:T(8,128)(2,1)S(1)} %get-tuple, ...), kind=kLoop, calls=%fused_computation.109 | loop fusion | bytes 19922944 | tf_op jit(solution)/shard_map/slice | solution.py:92
  89.3 2.6 fusion.29
  91.9 0.6 fusion.9
  92.5 1.7 pad_maximum_fusion
  94.2 0.6 fusion.8
  94.8 0.6 fusion.7
  95.4 2.2 pad_maximum_fusion.2
  97.6 0.6 fusion.6
  98.3 0.6 fusion.5
  98.9 2.1 pad_maximum_fusion.4
  101.0 0.6 fusion.4
  101.6 0.6 fusion.3
  102.3 2.2 pad_maximum_fusion.6
  104.5 0.6 fusion.2
  105.4 0.6 fusion.1
  106.0 1.2 copy-done.34
  107.3 1.9 copy.55
  109.6 1.0 copy-done
  111.4 1.0 copy-done.1
  112.8 1.0 copy-done.3
  114.2 1.0 copy-done.5
  115.6 1.0 copy-done.4
  118.9 0.7 pad_maximum_fusion.15
  128.7 0.6 copy-done.31
  132.3 0.6 convolution_add_fusion.15
  137.7 0.6 convolution_add_fusion.9
  139.4 0.6 convolution_add_fusion.7
  141.2 0.6 convolution_add_fusion.5
  143.0 0.6 convolution_add_fusion.3
  144.5 0.6 convolution_add_fusion.1
  145.1 0.6 convolution_add_fusion
  145.7 1.4 multiply_convert_fusion
  147.1 237.4 %all-reduce.5.cloned.1.call-done = f32[442368]{0:T(1024)} async-done(((f32[442368]{0:T(1024)}), f32[442368]{0:T(1024)}) %all-reduce.5.cloned.1.call-update) | async-done | bytes 1769488 | tf_op jit(solution)/shard_map/psum | solution.py:140
  384.4 1.4 dynamic-slice_multiply_fusion
  (188 shorter events, 27.0 us)
Async XLA Ops:
  7.2 24.3 %copy-start.6 = (bf16[27,128,128]{2,1,0:T(8,128)(2,1)S(1)}, bf16[27,128,128]{2,1,0:T(8,128)(2,1)}, u32[]{:S(2)}) copy-start(bf16[27,128,128]{2,1,0:T(8,128)(2,1)} %param.8) | copy-start | bytes 2654212
  7.2 377.3 %all-reduce.5.cloned.1.call-start = ((), (), s32[]{:S(2)}) async-start(), calls=%async_computation | async-start | bytes 3538944 | tf_op jit(solution)/shard_map/psum | solution.py:140
  9.1 26.6 %collective-permute-start.5 = (bf16[1,1,8,128]{3,1,2,0:T(2,128)(2,1)}, bf16[1,1,8,128]{3,1,2,0:T(2,128)(2,1)}, u32[]{:S(2)}, u32[]{:S(2)}) collective-permute-start(bf16[1,1,8,128]{3,1,2,0:T(2,128)(2,1)} %get-tuple-element.89), channel_id=1, source_target_pairs={{7,0},{8,1},{9,2},{10,3},{11,4},{12,5},{13,6},{14,7},{15,8},{16,9}... | collective-permute-start | bytes 6152 | tf_op jit(solution)/shard_map/ppermute | solution.py:24
  10.3 26.7 %collective-permute-start = (bf16[1,1,8,128]{3,1,2,0:T(2,128)(2,1)}, bf16[1,1,8,128]{3,1,2,0:T(2,128)(2,1)S(1)}, u32[]{:S(2)}, u32[]{:S(2)}) collective-permute-start(bf16[1,1,8,128]{3,1,2,0:T(2,128)(2,1)} %get-tuple-element.87), channel_id=1, source_target_pairs={{0,9},{1,10},{2,11},{3,12},{4,13},{5,14},{6,15},{7,16},{8,17},{9,1... | collective-permute-start | bytes 6152 | tf_op jit(solution)/shard_map/ppermute | solution.py:24
  20.3 27.8 %collective-permute-start.10 = (bf16[1,1,8,128]{3,1,2,0:T(2,128)(2,1)}, bf16[1,1,8,128]{3,1,2,0:T(2,128)(2,1)S(1)}, u32[]{:S(2)}, u32[]{:S(2)}) collective-permute-start(bf16[1,1,8,128]{3,1,2,0:T(2,128)(2,1)} %get-tuple-element.80), channel_id=1, source_target_pairs={{0,7},{1,8},{2,9},{3,10},{4,11},{5,12},{6,13},{7,14},{8,15},{9,16}... | collective-permute-start | bytes 6152 | tf_op jit(solution)/shard_map/ppermute | solution.py:24
  25.7 23.7 %collective-permute-start.7 = (bf16[1,1,8,128]{3,1,2,0:T(2,128)(2,1)}, bf16[1,1,8,128]{3,1,2,0:T(2,128)(2,1)S(1)}, u32[]{:S(2)}, u32[]{:S(2)}) collective-permute-start(bf16[1,1,8,128]{3,1,2,0:T(2,128)(2,1)} %get-tuple-element.88), channel_id=1, source_target_pairs={{9,0},{10,1},{11,2},{12,3},{13,4},{14,5},{15,6},{16,7},{17,8},{18,... | collective-permute-start | bytes 6152 | tf_op jit(solution)/shard_map/ppermute | solution.py:24
  27.0 23.8 %collective-permute-start.2 = (bf16[1,1,8,128]{3,1,2,0:T(2,128)(2,1)}, bf16[1,1,8,128]{3,1,2,0:T(2,128)(2,1)S(1)}, u32[]{:S(2)}, u32[]{:S(2)}) collective-permute-start(bf16[1,1,8,128]{3,1,2,0:T(2,128)(2,1)} %get-tuple-element.90), channel_id=1, source_target_pairs={{0,7},{1,8},{2,9},{3,10},{4,11},{5,12},{6,13},{7,14},{8,15},{9,16}... | collective-permute-start | bytes 6152 | tf_op jit(solution)/shard_map/ppermute | solution.py:24
  31.5 2.3 copy-start.60
  32.5 2.8 copy-start.51
  33.8 1.9 copy-start.59
  33.8 3.2 copy-start.58
  33.8 14.3 %copy-start.57 = (bf16[1,1,8,128]{3,1,2,0:T(2,128)(2,1)S(1)}, bf16[1,1,8,128]{3,1,2,0:T(2,128)(2,1)}, u32[]{:S(2)}) copy-start(bf16[1,1,8,128]{3,1,2,0:T(2,128)(2,1)} %get-tuple-element.78) | copy-start | bytes 6148
  33.8 15.6 %copy-start.54 = (bf16[16,1,8,128]{3,1,2,0:T(2,128)(2,1)S(1)}, bf16[16,1,8,128]{3,1,2,0:T(2,128)(2,1)}, u32[]{:S(2)}) copy-start(bf16[16,1,8,128]{3,1,2,0:T(2,128)(2,1)} %get-tuple-element.84) | copy-start | bytes 98308
  33.8 17.0 %copy-start.53 = (bf16[16,1,8,128]{3,1,2,0:T(2,128)(2,1)S(1)}, bf16[16,1,8,128]{3,1,2,0:T(2,128)(2,1)}, u32[]{:S(2)}) copy-start(bf16[16,1,8,128]{3,1,2,0:T(2,128)(2,1)} %get-tuple-element.94) | copy-start | bytes 98308
  33.8 18.3 %copy-start.52 = (bf16[16,1,8,128]{3,1,2,0:T(2,128)(2,1)S(1)}, bf16[16,1,8,128]{3,1,2,0:T(2,128)(2,1)}, u32[]{:S(2)}) copy-start(bf16[16,1,8,128]{3,1,2,0:T(2,128)(2,1)} %get-tuple-element.83) | copy-start | bytes 98308
  34.1 26.1 %copy-start.56 = (bf16[1,16,8,128]{3,1,2,0:T(8,128)(2,1)S(1)}, bf16[1,16,8,128]{3,1,2,0:T(8,128)(2,1)}, u32[]{:S(2)}) copy-start(bf16[1,16,8,128]{3,1,2,0:T(8,128)(2,1)} %get-tuple-element.91) | copy-start | bytes 98308
  34.2 32.7 %copy-start.55 = (bf16[1,16,8,128]{3,1,2,0:T(8,128)(2,1)S(1)}, bf16[1,16,8,128]{3,1,2,0:T(8,128)(2,1)}, u32[]{:S(2)}) copy-start(bf16[1,16,8,128]{3,1,2,0:T(8,128)(2,1)} %get-tuple-element.92) | copy-start | bytes 98308
  35.7 16.4 %collective-permute-start.13 = (bf16[1,1,8,128]{3,1,2,0:T(2,128)(2,1)S(1)}, bf16[1,1,8,128]{3,1,2,0:T(2,128)(2,1)S(1)}, u32[]{:S(2)}, u32[]{:S(2)}) collective-permute-start(bf16[1,1,8,128]{3,1,2,0:T(2,128)(2,1)S(1)} %copy-done.59), channel_id=1, source_target_pairs={{7,0},{8,1},{9,2},{10,3},{11,4},{12,5},{13,6},{14,7},{15,8},{16,9}... | collective-permute-start | bytes 6152 | tf_op jit(solution)/shard_map/ppermute | solution.py:24
  37.0 19.8 %collective-permute-start.8 = (bf16[1,1,8,128]{3,1,2,0:T(2,128)(2,1)S(1)}, bf16[1,1,8,128]{3,1,2,0:T(2,128)(2,1)S(1)}, u32[]{:S(2)}, u32[]{:S(2)}) collective-permute-start(bf16[1,1,8,128]{3,1,2,0:T(2,128)(2,1)S(1)} %copy-done.58), channel_id=1, source_target_pairs={{0,9},{1,10},{2,11},{3,12},{4,13},{5,14},{6,15},{7,16},{8,17},{9,1... | collective-permute-start | bytes 6152 | tf_op jit(solution)/shard_map/ppermute | solution.py:24
  48.1 12.1 %collective-permute-start.15 = (bf16[1,1,8,128]{3,1,2,0:T(2,128)(2,1)S(1)}, bf16[1,1,8,128]{3,1,2,0:T(2,128)(2,1)S(1)}, u32[]{:S(2)}, u32[]{:S(2)}) collective-permute-start(bf16[1,1,8,128]{3,1,2,0:T(2,128)(2,1)S(1)} %copy-done.57), channel_id=1, source_target_pairs={{9,0},{10,1},{11,2},{12,3},{13,4},{14,5},{15,6},{16,7},{17,8},{18,... | collective-permute-start | bytes 6152 | tf_op jit(solution)/shard_map/ppermute | solution.py:24
  49.5 16.1 %collective-permute-start.12 = (bf16[16,1,8,128]{3,1,2,0:T(2,128)(2,1)S(1)}, bf16[16,1,8,128]{3,1,2,0:T(2,128)(2,1)S(1)}, u32[]{:S(2)}, u32[]{:S(2)}) collective-permute-start(bf16[16,1,8,128]{3,1,2,0:T(2,128)(2,1)S(1)} %copy-done.54), channel_id=1, source_target_pairs={{1,0},{2,1},{3,2},{4,3},{5,4},{6,5},{7,6},{8,7},{9,8},{10,9},{11,1... | collective-permute-start | bytes 98312 | tf_op jit(solution)/shard_map/ppermute | solution.py:24
  50.8 16.1 %collective-permute-start.4 = (bf16[16,1,8,128]{3,1,2,0:T(2,128)(2,1)S(1)}, bf16[16,1,8,128]{3,1,2,0:T(2,128)(2,1)S(1)}, u32[]{:S(2)}, u32[]{:S(2)}) collective-permute-start(bf16[16,1,8,128]{3,1,2,0:T(2,128)(2,1)S(1)} %copy-done.53), channel_id=1, source_target_pairs={{1,0},{2,1},{3,2},{4,3},{5,4},{6,5},{7,6},{8,7},{9,8},{10,9},{11,1... | collective-permute-start | bytes 98312 | tf_op jit(solution)/shard_map/ppermute | solution.py:24
  52.1 16.2 %collective-permute-start.11 = (bf16[16,1,8,128]{3,1,2,0:T(2,128)(2,1)S(1)}, bf16[16,1,8,128]{3,1,2,0:T(2,128)(2,1)S(1)}, u32[]{:S(2)}, u32[]{:S(2)}) collective-permute-start(bf16[16,1,8,128]{3,1,2,0:T(2,128)(2,1)S(1)} %copy-done.52), channel_id=1, source_target_pairs={{0,1},{1,2},{2,3},{3,4},{4,5},{5,6},{6,7},{7,8},{8,9},{9,10},{10,1... | collective-permute-start | bytes 98312 | tf_op jit(solution)/shard_map/ppermute | solution.py:24
  56.8 19.4 %collective-permute-start.3 = (bf16[16,1,8,128]{3,1,2,0:T(2,128)(2,1)S(1)}, bf16[16,1,8,128]{3,1,2,0:T(2,128)(2,1)S(1)}, u32[]{:S(2)}, u32[]{:S(2)}) collective-permute-start(bf16[16,1,8,128]{3,1,2,0:T(2,128)(2,1)S(1)} %get-tuple-element.93), channel_id=1, source_target_pairs={{0,1},{1,2},{2,3},{3,4},{4,5},{5,6},{6,7},{7,8},{8,9},{9,10},{10,1... | collective-permute-start | bytes 98312 | tf_op jit(solution)/shard_map/ppermute | solution.py:24
  60.3 16.0 %collective-permute-start.1 = (bf16[1,16,8,128]{3,1,2,0:T(8,128)(2,1)S(1)}, bf16[1,16,8,128]{3,1,2,0:T(8,128)(2,1)S(1)}, u32[]{:S(2)}, u32[]{:S(2)}) collective-permute-start(bf16[1,16,8,128]{3,1,2,0:T(8,128)(2,1)S(1)} %copy-done.56), channel_id=1, source_target_pairs={{0,8},{1,9},{2,10},{3,11},{4,12},{5,13},{6,14},{7,15},{8,16},{9,17... | collective-permute-start | bytes 98312 | tf_op jit(solution)/shard_map/ppermute | solution.py:24
  65.5 10.8 %collective-permute-start.14 = (bf16[1,16,8,128]{3,1,2,0:T(8,128)(2,1)S(1)}, bf16[1,16,8,128]{3,1,2,0:T(8,128)(2,1)S(1)}, u32[]{:S(2)}, u32[]{:S(2)}) collective-permute-start(bf16[1,16,8,128]{3,1,2,0:T(8,128)(2,1)S(1)} %get-tuple-element.82), channel_id=1, source_target_pairs={{8,0},{9,1},{10,2},{11,3},{12,4},{13,5},{14,6},{15,7},{16,8},{17,9... | collective-permute-start | bytes 98312 | tf_op jit(solution)/shard_map/ppermute | solution.py:24
  66.9 9.4 %collective-permute-start.6 = (bf16[1,16,8,128]{3,1,2,0:T(8,128)(2,1)S(1)}, bf16[1,16,8,128]{3,1,2,0:T(8,128)(2,1)S(1)}, u32[]{:S(2)}, u32[]{:S(2)}) collective-permute-start(bf16[1,16,8,128]{3,1,2,0:T(8,128)(2,1)S(1)} %copy-done.55), channel_id=1, source_target_pairs={{8,0},{9,1},{10,2},{11,3},{12,4},{13,5},{14,6},{15,7},{16,8},{17,9... | collective-permute-start | bytes 98312 | tf_op jit(solution)/shard_map/ppermute | solution.py:24
  68.3 8.8 %collective-permute-start.9 = (bf16[1,16,8,128]{3,1,2,0:T(8,128)(2,1)S(1)}, bf16[1,16,8,128]{3,1,2,0:T(8,128)(2,1)S(1)}, u32[]{:S(2)}, u32[]{:S(2)}) collective-permute-start(bf16[1,16,8,128]{3,1,2,0:T(8,128)(2,1)S(1)} %get-tuple-element.81), channel_id=1, source_target_pairs={{0,8},{1,9},{2,10},{3,11},{4,12},{5,13},{6,14},{7,15},{8,16},{9,17... | collective-permute-start | bytes 98312 | tf_op jit(solution)/shard_map/ppermute | solution.py:24
  106.0 1.3 copy-start.34
  107.3 1.9 copy-start.2
  109.2 1.4 copy-start
  111.0 1.4 copy-start.1
  112.4 1.4 copy-start.3
  113.8 1.4 copy-start.5
  115.2 1.4 copy-start.4
  117.0 1.0 copy-start.25
  117.1 1.2 copy-start.26
  117.1 1.3 copy-start.27
  117.1 1.5 copy-start.28
  117.1 1.6 copy-start.29
  117.1 1.8 copy-start.30
  119.6 1.0 copy-start.19
  119.6 1.2 copy-start.20
  119.6 1.3 copy-start.21
  119.7 1.5 copy-start.22
  119.7 1.6 copy-start.23
  119.7 1.8 copy-start.24
  122.0 1.0 copy-start.13
  122.0 1.2 copy-start.14
  122.0 1.3 copy-start.15
  122.0 1.5 copy-start.16
  122.0 1.6 copy-start.17
  122.0 1.8 copy-start.18
  124.4 1.0 copy-start.7
  124.4 1.2 copy-start.8
  124.4 1.3 copy-start.9
  124.4 1.5 copy-start.10
  124.4 1.6 copy-start.11
  124.4 1.8 copy-start.12
  128.3 1.0 copy-start.31
  128.3 1.2 copy-start.32
  128.3 1.3 copy-start.33
  130.3 1.1 copy-start.50
  135.9 0.9 copy-start.41
  (14 other events, 12.5 us)
Sparse Core Ops, SparseCore 0:
  107.4 276.9 all-reduce.4
where the time goes:
time: 395 us; the launch traced here: 393 us
  waiting for transfers between devices  238 us (60%)
  starting transfers between devices  58.4 us (15%)
  local copies, waits for them, and re-layouts  45.9 us (12%)
  other arithmetic  18.9 us (5%)
  matrix products  16 us (4%)
  between operations  15.3 us (4%)
    psum x1, waiting for transfers between devices, body(): summed = lax.psum(weight_flat, ('dp', 'block'))  237 us
    ppermute x16, starting transfers between devices, passed_along(): lax.ppermute(value, axis, [(source, source + steps) for source in range(f...  58.4 us
    unnamed x125, local copies, waits for them, and re-layouts  21.3 us
    concatenate x5, other arithmetic, convolve(): jnp.concatenate([feat_full[..., shift_x:shift_x + extent_x, shift_y:shift...  8.5 us
  transfers between devices with their start and end apart: 17, of which 2 were waited for; matrix products, arithmetic and copies ran while one was open for 8% of the time, Pallas kernels for 0%

commit v1 on v0

v1 whole, which is shorter than its diff:
```python
import functools
import math

import jax
import jax.numpy as jnp
from jax import lax
from jax.experimental import pallas as pl
from jax.experimental.pallas import tpu as pltpu
from jax.sharding import PartitionSpec as P

MESH = pl.DeviceIdType.MESH
BF = jnp.bfloat16
F32 = jnp.float32

C = 128
LX, LY, LZ = 16, 16, 8
GX, GY = 16, 8
NX, NY, NZ = 4, 4, 8
SHARE = 27
HALF = 16
CHUNKS = ((0, 2), (2, 5), (5, 8))
DIRS = [(dx, dy) for dx in (-1, 0, 1) for dy in (-1, 0, 1) if (dx, dy) != (0, 0)]


def kernel(
    f_hbm, g_hbm, mask_ref, list_ref, w_ref,
    out_hbm, ig_hbm, wg_ref,
    cells, halo_x, halo_y, active, fb, gb, g3, dw, pack, landed, t_sum, r1, u_sum, r2, v_sum, r3, fin, conv_out,
    in_sem, halo_send, halo_recv, dp_send, dp_recv, s1_send, s1_recv, s2_send, s2_recv, s3_send, s3_recv,
    fin_send, fin_recv, out_sem,
):
    core = lax.axis_index("dp")
    me = lax.axis_index("block")
    chip_z, chip_y, chip_x = me // 16, (me // 4) % 4, me % 4
    block_x, block_y = me // GY, me % GY
    first, second = 1 + 3 * core, 4 - 3 * core
    my_p = chip_x + core * (chip_y - chip_x)
    my_q = chip_y + core * (chip_x - chip_y)
    sources = (f_hbm, g_hbm)

    loads = [pltpu.make_async_copy(src, cells.at[i], in_sem.at[i]) for i, src in enumerate(sources)]
    for load in loads:
        load.start()

    def beside(dx, dy):
        return (core, ((block_x + dx + GX) % GX) * GY + (block_y + dy + GY) % GY)

    def along_p(k):
        return (core, 16 * chip_z + first * ((my_p + k) % 4) + second * my_q)

    def along_q(k):
        return (core, 16 * chip_z + first * my_p + second * ((my_q + k) % 4))

    def along_z(k):
        return (core, 16 * ((chip_z + k) % 8) + me % 16)

    sibling = (1 - core, me)

    barrier = pltpu.get_barrier_semaphore()
    partners = [beside(dx, dy) for dx, dy in DIRS]
    partners += [along_p(k) for k in (1, 2, 3)] + [along_q(k) for k in (1, 2, 3)] + [along_z(k) for k in range(1, 8)]
    partners.append(sibling)
    for partner in partners:
        pl.semaphore_signal(barrier, inc=1, device_id=partner, device_id_type=MESH)
    pl.semaphore_wait(barrier, len(partners))

    def remote(src, dst, send, recv, device):
        return pltpu.make_async_remote_copy(
            src_ref=src, dst_ref=dst, send_sem=send, recv_sem=recv, device_id=device, device_id_type=MESH
        )

    halos = []
    for i, src in enumerate(sources):
        copies = []
        for n, (dx, dy) in enumerate(DIRS):
            row = LX - 1 if dx == 1 else 0
            col = LY - 1 if dy == 1 else 0
            side_x = 0 if dx == 1 else 1
            side_y = 0 if dy == 1 else 1
            if dx == 0:
                a, b = src.at[:, col], halo_y.at[i, side_y]
            elif dy == 0:
                a, b = src.at[row], halo_x.at[i, side_x, 1:17]
            else:
                a, b = src.at[row, col], halo_x.at[i, side_x, 0 if dy == 1 else 17]
            copies.append(remote(a, b, halo_send.at[i, n], halo_recv.at[i, n], beside(dx, dy)))
        for copy in copies:
            copy.start()
        halos.append(copies)

    dw[3456:3464, :] = jnp.zeros((8, C), F32)

    rows_y = lax.broadcasted_iota(jnp.int32, (144, 18), 0) // 8
    pick_y = (rows_y == lax.broadcasted_iota(jnp.int32, (144, 18), 1)).astype(F32)
    rows_z = lax.broadcasted_iota(jnp.int32, (144, 10), 0) % 8 + 1
    pick_z = (rows_z == lax.broadcasted_iota(jnp.int32, (144, 10), 1)).astype(BF)
    spread = jnp.ones((18, C), BF)
    at_z = lax.broadcasted_iota(jnp.int32, (10, 18), 0)
    at_y = lax.broadcasted_iota(jnp.int32, (10, 18), 1)
    entries = [list_ref[0, n] for n in range(4)]

    def is_listed(brick):
        hit = entries[0] == brick
        for entry in entries[1:]:
            hit = jnp.logical_or(hit, entry == brick)
        return jnp.where(hit, 1, 0)

    def listing_of(half):
        s = [is_listed(4 * half + n) for n in range(4)]
        low = jnp.where(at_z < 5, s[0], s[1])
        high = jnp.where(at_z < 5, s[2], s[3])
        inner = jnp.where(at_y < 9, low, high)
        edge = jnp.logical_or(at_y == 0, at_y == 17)
        return jnp.where(edge, 1, inner)

    halves = [listing_of(0), listing_of(1)]

    def mask_slab(x, listing):
        plane = mask_ref[x]
        if listing is not None:
            plane = plane * listing
        by_z = jnp.dot(pick_z, plane.astype(BF), preferred_element_type=F32)
        spread_out = jnp.dot((by_z * pick_y).astype(BF), spread, preferred_element_type=F32)
        active[x] = spread_out.reshape(18, LZ, C)

    mask_slab(0, None)
    mask_slab(17, None)
    for half in range(2):
        def mask_step(n, carry, half=half):
            mask_slab(1 + 8 * half + n, halves[half])
            return carry
        lax.fori_loop(0, 8, mask_step, 0, unroll=8)

    z_at = lax.broadcasted_iota(jnp.int32, (LY, LZ, C), 1)
    for load in loads:
        load.wait()

    def g3_step(x, carry):
        value = cells[1, x].astype(F32) * active[x + 1, 1:17]
        after = jnp.where(z_at < LZ - 1, pltpu.roll(value, LZ - 1, 1), 0.0)
        before = jnp.where(z_at > 0, pltpu.roll(value, 1, 1), 0.0)
        for c, part in enumerate((after, value, before)):
            g3[x, :, c * C : (c + 1) * C] = part.reshape(128, C).astype(BF)
        return carry

    lax.fori_loop(0, LX, g3_step, 0, unroll=2)

    def columns(i, dst):
        def put(x, slab):
            value = slab.astype(F32) * active[x]
            for b in range(3):
                dst[x, :, b * C : (b + 1) * C] = value[b : b + 16].reshape(128, C).astype(BF)

        def step(x, carry):
            put(x + 1, jnp.concatenate([halo_y[i, 0, pl.ds(x, 1)], cells[i, x], halo_y[i, 1, pl.ds(x, 1)]], axis=0))
            return carry

        put(0, halo_x[i, 0])
        put(17, halo_x[i, 1])
        lax.fori_loop(0, LX, step, 0, unroll=2)

    for copy in halos[0]:
        copy.wait_recv()
    columns(0, fb)

    def weight_third(a):
        lhs = fb[a : a + LX].reshape(2048, 3 * C)
        got = lax.dot_general(lhs, g3[...].reshape(2048, 3 * C), (((0,), (0,)), ((), ())), preferred_element_type=F32)
        for b in range(3):
            for c in range(3):
                row = (9 * a + 3 * b + c) * C
                dw[row : row + C, :] = got[b * C : (b + 1) * C, c * C : (c + 1) * C]

    dp_copies = []

    def each(lo, hi, body):
        lax.fori_loop(lo, hi, lambda n, carry: (body(n), carry)[1], 0, unroll=8)

    def send_pair(n):
        lo, hi = CHUNKS[n]

        def body(i):
            z, p, q = i // 16, (i // 4) % 4, i % 4
            start = SHARE * (16 * z + second * p + first * q) + HALF * (1 - core)
            pack[z, p, q] = dw[pl.ds(start, HALF), :]

        each(16 * lo, 16 * hi, body)
        copy = remote(pack.at[lo:hi], landed.at[lo:hi], dp_send.at[n], dp_recv.at[n], sibling)
        copy.start()
        dp_copies.append(copy)

    s1_copies, s2_copies = [], []

    def add_pair(n):
        lo, hi = CHUNKS[n]
        dp_copies[n].wait_recv()

        def body(i):
            z, p, q = i // 16, (i // 4) % 4, i % 4
            start = SHARE * (16 * z + first * p + second * q) + HALF * core
            t_sum[z, p, q] = dw[pl.ds(start, HALF), :] + landed[z, p, q]

        each(16 * lo, 16 * hi, body)
        copies = [
            remote(
                t_sum.at[lo:hi, (my_p + k) % 4], r1.at[k - 1, lo:hi],
                s1_send.at[n, k - 1], s1_recv.at[n, k - 1], along_p(k),
            )
            for k in (1, 2, 3)
        ]
        for copy in copies:
            copy.start()
        s1_copies.append(copies)

    def add_first(n):
        lo, hi = CHUNKS[n]
        for copy in s1_copies[n]:
            copy.wait_recv()
        for z in range(lo, hi):
            u_sum[z] = (t_sum[z, my_p] + r1[0, z]) + (r1[1, z] + r1[2, z])
        copies = [
            remote(
                u_sum.at[lo:hi, (my_q + k) % 4], r2.at[k - 1, lo:hi],
                s2_send.at[n, k - 1], s2_recv.at[n, k - 1], along_q(k),
            )
            for k in (1, 2, 3)
        ]
        for copy in copies:
            copy.start()
        s2_copies.append(copies)

    def add_second(n):
        lo, hi = CHUNKS[n]
        for copy in s2_copies[n]:
            copy.wait_recv()
        for z in range(lo, hi):
            v_sum[z] = (u_sum[z, my_q] + r2[0, z]) + (r2[1, z] + r2[2, z])

    z_row = lax.broadcasted_iota(jnp.int32, (128, LZ, C), 1)
    out_copies = []

    def convolve(i, x0):
        src = (fb, gb)[i]
        lhs = jnp.concatenate([src[x0 + a : x0 + a + 8].reshape(1024, 3 * C) for a in range(3)], axis=1)
        if i == 0:
            rhs = jnp.concatenate(
                [jnp.concatenate([w_ref[3 * ab + c] for c in range(3)], axis=1) for ab in range(9)], axis=0
            )
            acc = jnp.dot(lhs, rhs, preferred_element_type=F32)
        else:
            rhs = jnp.concatenate(
                [jnp.concatenate([w_ref[26 - 3 * ab - c] for ab in range(9)], axis=1) for c in range(3)], axis=0
            )
            acc = lax.dot_general(lhs, rhs, (((1,), (1,)), ((), ())), preferred_element_type=F32)
        acc = acc.reshape(128, LZ, 3 * C)
        low = jnp.where(z_row > 0, pltpu.roll(acc[:, :, :C], 1, 1), 0.0)
        high = jnp.where(z_row < LZ - 1, pltpu.roll(acc[:, :, 2 * C :], LZ - 1, 1), 0.0)
        inside = active[x0 + 1 : x0 + 9, 1:17].reshape(128, LZ, C)
        value = (acc[:, :, C : 2 * C] + low + high) * inside
        conv_out[i, x0 : x0 + 8] = value.astype(BF).reshape(8, LY, LZ, C)
        copy = pltpu.make_async_copy(
            conv_out.at[i, x0 : x0 + 8], (out_hbm, ig_hbm)[i].at[x0 : x0 + 8], out_sem.at[i, x0 // 8]
        )
        copy.start()
        out_copies.append(copy)

    weight_third(0)
    send_pair(0)
    weight_third(1)
    send_pair(1)
    add_pair(0)
    weight_third(2)
    send_pair(2)
    add_pair(1)
    for copy in halos[1]:
        copy.wait_recv()
    columns(1, gb)
    add_pair(2)
    convolve(0, 0)
    add_first(0)
    add_first(1)
    convolve(0, 8)
    add_first(2)
    convolve(1, 0)
    add_second(0)
    add_second(1)
    add_second(2)
    s3_copies = [
        remote(v_sum.at[(chip_z + k) % 8], r3.at[k - 1], s3_send.at[k - 1], s3_recv.at[k - 1], along_z(k))
        for k in range(1, 8)
    ]
    for copy in s3_copies:
        copy.start()
    convolve(1, 8)
    for copy in s3_copies:
        copy.wait_recv()
    total = v_sum[chip_z]
    for k in range(7):
        total = total + r3[k]
    fin[core] = total * (1.0 / math.sqrt(2 * 128 * LX * LY * LZ))
    last = remote(fin.at[core], fin.at[core], fin_send, fin_recv, sibling)
    last.start()

    for copies in halos + s1_copies + s2_copies + [dp_copies, s3_copies]:
        for copy in copies:
            copy.wait_send()
    for copy in out_copies:
        copy.wait()
    last.wait()
    wg_ref[0:HALF, :] = fin[0]
    wg_ref[HALF:SHARE, :] = fin[1, 0 : SHARE - HALF]


def body(features, mask_margin, brick_list, kernel_weight, cotangent):
    any_spec = pl.BlockSpec(memory_space=pl.ANY)
    vmem = pl.BlockSpec(memory_space=pltpu.VMEM)
    mask = jnp.transpose(mask_margin[0, 0], (0, 2, 1))
    block = (LX, LY, LZ, C)
    dma = pltpu.SemaphoreType.DMA
    output, input_grad, share = pl.pallas_call(
        kernel,
        name="conv_and_grads",
        out_shape=(
            jax.ShapeDtypeStruct(block, BF),
            jax.ShapeDtypeStruct(block, BF),
            jax.ShapeDtypeStruct((SHARE, C), F32),
        ),
        in_specs=[any_spec, any_spec, vmem, pl.BlockSpec(memory_space=pltpu.SMEM), vmem],
        out_specs=(any_spec, any_spec, vmem),
        scratch_shapes=[
            pltpu.VMEM((2,) + block, BF),
            pltpu.VMEM((2, 2, 18, LZ, C), BF),
            pltpu.VMEM((2, 2, LX, LZ, C), BF),
            pltpu.VMEM((18, 18, LZ, C), F32),
            pltpu.VMEM((18, 128, 3 * C), BF),
            pltpu.VMEM((18, 128, 3 * C), BF),
            pltpu.VMEM((16, 128, 3 * C), BF),
            pltpu.VMEM((3464, C), F32),
            pltpu.VMEM((8, 4, 4, HALF, C), F32),
            pltpu.VMEM((8, 4, 4, HALF, C), F32),
            pltpu.VMEM((8, 4, 4, HALF, C), F32),
            pltpu.VMEM((3, 8, 4, HALF, C), F32),
            pltpu.VMEM((8, 4, HALF, C), F32),
            pltpu.VMEM((3, 8, HALF, C), F32),
            pltpu.VMEM((8, HALF, C), F32),
            pltpu.VMEM((7, HALF, C), F32),
            pltpu.VMEM((2, HALF, C), F32),
            pltpu.VMEM((2,) + block, BF),
            dma((2,)),
            dma((2, 8)), dma((2, 8)),
            dma((3,)), dma((3,)),
            dma((3, 3)), dma((3, 3)),
            dma((3, 3)), dma((3, 3)),
            dma((7,)), dma((7,)),
            dma, dma,
            dma((2, 2)),
        ],
        compiler_params=pltpu.CompilerParams(
            collective_id=0, has_side_effects=True, vmem_limit_bytes=48 * 1024 * 1024
        ),
    )(features[0, 0], cotangent[0, 0], mask, brick_list[0], kernel_weight)
    return output[None, None], input_grad[None, None], share.reshape(-1)


def solution(mesh):
    tile = P("dp", "block")
    return jax.shard_map(
        body,
        mesh=mesh,
        in_specs=(tile, tile, tile, P(), tile),
        out_specs=(tile, tile, P("block")),
        check_vma=False,
    )
```

time: 395 us -> 50.4 us (0.13)
  waiting for transfers between devices: 238 us -> 0 us
  starting transfers between devices: 58.4 us -> 0 us
  Pallas kernels: 0 us -> 42.5 us
  local copies, waits for them, and re-layouts: 45.9 us -> 7 us
  other arithmetic: 18.9 us -> 0 us
  matrix products: 16 us -> 0 us
  between operations: 15.3 us -> 0.65 us
    psum x1 -> x0, waiting for transfers between devices: 237 us -> none  [body(): summed = lax.psum(weight_flat, ('dp', 'block'))]
    ppermute x16 -> x0, starting transfers between devices: 58.4 us -> none  [passed_along(): lax.ppermute(value, axis, [(source, source + steps) for source in range(f...]
    pallas_call x0 -> x1, Pallas kernels: none -> 42.5 us  [body(): pl.pallas_call(kernel, name='conv_and_grads', out_shape=(jax.ShapeDtypeSt...]
    dot_general x27 -> x0, matrix products: 16 us -> none  [the longest x9 5.51 us: convolve(): lax.dot_general(feat_stack, inside_grad, (((0,), (0,)), ((), ())), prefer...]
    slice x12 -> x0, local copies, waits for them, and re-layouts: 15.6 us -> none  [the longest x2 6.86 us: convolve(): grad_full[..., 2 - shift_x:2 - shift_x + extent_x, 2 - shift_y:2 - shift_...]
    unnamed x125 -> x11, local copies, waits for them, and re-layouts: 21.3 us -> 6.09 us
    concatenate x10 -> x0, other arithmetic: 11 us -> none  [the longest x5 8.5 us: convolve(): jnp.concatenate([feat_full[..., shift_x:shift_x + extent_x, shift_y:shift...]
    concatenate x18 -> x0, local copies, waits for them, and re-layouts: 8.47 us -> none  [the longest x9 4.99 us: convolve(): jnp.concatenate([feat_full[..., shift_x:shift_x + extent_x, shift_y:shift...]
  transfers between devices with their start and end apart: 17 -> 0, of which waited for: 2 -> 0; matrix products, arithmetic and copies ran while one was open for 8% -> 0% of each run, Pallas kernels for 0% -> 0%
where the time goes in v1:
time: 50.4 us; the launch traced here: 50.1 us
  Pallas kernels  42.5 us (84%)
  local copies, waits for them, and re-layouts  7 us (14%)
  between operations  0.65 us (1%)
    pallas_call x1, Pallas kernels, body(): pl.pallas_call(kernel, name='conv_and_grads', out_shape=(jax.ShapeDtypeSt...  42.5 us
    unnamed x11, local copies, waits for them, and re-layouts  6.09 us

profile of v1, /device:TPU:1, one launch (start us, length us, event | category | flops | bytes accessed | tf_op | source)
XLA Modules:
  0.0 50.1 jit_solution(851590775774400855)
XLA Ops:
  0.6 0.9 %copy.12 = s32[1,1,18,18,10]{3,4,2,0,1:T(8,128)S(1)} copy(s32[1,1,18,18,10]{3,1,4,2,0:T(1,128)} %param.6) | data formatting | bytes 25920 | tf_op jit(solution)/shard_map/squeeze | solution.py:317
  1.5 0.0 copy-start.3
  1.6 0.6 %copy-done.3 = s32[1,1,4]{2,1,0:T(1,128)S(1)} copy-done((s32[1,1,4]{2,1,0:T(1,128)S(1)}, s32[1,1,4]{2,1,0:T(1,128)}, u32[]{:S(2)}) %copy-start.3) | copy-done | bytes 40
  2.2 0.0 copy-start
  2.2 1.2 %copy-done = bf16[27,128,128]{2,1,0:T(8,128)(2,1)S(1)} copy-done((bf16[27,128,128]{2,1,0:T(8,128)(2,1)S(1)}, bf16[27,128,128]{2,1,0:T(8,128)(2,1)}, u32[]{:S(2)}) %copy-start) | copy-done | bytes 884760
  3.4 0.0 copy-start.1
  3.4 1.0 %copy-done.1 = bf16[1,1,16,16,8,128]{5,4,3,2,1,0:T(8,128)(2,1)S(1)} copy-done((bf16[1,1,16,16,8,128]{5,4,3,2,1,0:T(8,128)(2,1)S(1)}, bf16[1,1,16,16,8,128]{5,4,3,2,1,0:T(8,128)(2,1)}, u32[]{:S(2)}) %copy-start.1) | copy-done | bytes 524312
  4.4 0.0 copy-start.2
  4.4 1.0 %copy-done.2 = bf16[1,1,16,16,8,128]{5,4,3,2,1,0:T(8,128)(2,1)S(1)} copy-done((bf16[1,1,16,16,8,128]{5,4,3,2,1,0:T(8,128)(2,1)S(1)}, bf16[1,1,16,16,8,128]{5,4,3,2,1,0:T(8,128)(2,1)}, u32[]{:S(2)}) %copy-start.2) | copy-done | bytes 524312
  5.4 42.5 %conv_and_grads.1 = (bf16[16,16,8,128]{3,2,1,0:T(8,128)(2,1)S(1)}, bf16[16,16,8,128]{3,2,1,0:T(8,128)(2,1)S(1)}, f32[27,128]{1,0:T(8,128)S(1)}) custom-call(bf16[16,16,8,128]{3,2,1,0:T(8,128)(2,1)S(1)} %bitcast.13, bf16[16,16,8,128]{3,2,1,0:T(8,128)(2,1)S(1)} %bitcast.14, s32[18,10,18]{2,1,0:T(8,128)S(1)} %bitcast.12, s32[1,4]{1,0:T(1,128)S(1)} %bitcast.18, ...), custom_call_target="tpu_custom_call" | custom-call | tf_op jit(solution)/shard_map/conv_and_grads/pallas_call | solution.py:320
  47.9 0.8 %copy.16 = bf16[1,1,16,16,8,128]{5,4,3,2,1,0:T(8,128)(2,1)} copy(bf16[1,1,16,16,8,128]{5,4,3,2,1,0:T(8,128)(2,1)S(1)} %bitcast.16) | data formatting | bytes 1048576
  48.7 0.8 %copy.17 = bf16[1,1,16,16,8,128]{5,4,3,2,1,0:T(8,128)(2,1)} copy(bf16[1,1,16,16,8,128]{5,4,3,2,1,0:T(8,128)(2,1)S(1)} %bitcast.15) | data formatting | bytes 1048576
  49.5 0.6 %copy.18 = f32[3456]{0:T(1024)} copy(f32[3456]{0:T(1024)S(1)} %bitcast.17) | data formatting | bytes 27648
Async XLA Ops:
  1.5 0.7 %copy-start.3 = (s32[1,1,4]{2,1,0:T(1,128)S(1)}, s32[1,1,4]{2,1,0:T(1,128)}, u32[]{:S(2)}) copy-start(s32[1,1,4]{2,1,0:T(1,128)} %param.7) | copy-start | bytes 52
  2.2 1.2 %copy-start = (bf16[27,128,128]{2,1,0:T(8,128)(2,1)S(1)}, bf16[27,128,128]{2,1,0:T(8,128)(2,1)}, u32[]{:S(2)}) copy-start(bf16[27,128,128]{2,1,0:T(8,128)(2,1)} %w_ref.1) | copy-start | bytes 2654212
  3.4 1.0 %copy-start.1 = (bf16[1,1,16,16,8,128]{5,4,3,2,1,0:T(8,128)(2,1)S(1)}, bf16[1,1,16,16,8,128]{5,4,3,2,1,0:T(8,128)(2,1)}, u32[]{:S(2)}) copy-start(bf16[1,1,16,16,8,128]{5,4,3,2,1,0:T(8,128)(2,1)} %param.5) | copy-start | bytes 1572868
  4.4 1.0 %copy-start.2 = (bf16[1,1,16,16,8,128]{5,4,3,2,1,0:T(8,128)(2,1)S(1)}, bf16[1,1,16,16,8,128]{5,4,3,2,1,0:T(8,128)(2,1)}, u32[]{:S(2)}) copy-start(bf16[1,1,16,16,8,128]{5,4,3,2,1,0:T(8,128)(2,1)} %param.9) | copy-start | bytes 1572868

commit v2 on v1

v2 whole, which is shorter than its diff:
```python
import functools
import math

import jax
import jax.numpy as jnp
from jax import lax
from jax.experimental import pallas as pl
from jax.experimental.pallas import tpu as pltpu
from jax.sharding import PartitionSpec as P

MESH = pl.DeviceIdType.MESH
BF = jnp.bfloat16
F32 = jnp.float32

C = 128
LX, LY, LZ = 16, 16, 8
GX, GY = 16, 8
NX, NY, NZ = 4, 4, 8
SHARE = 27
HALF = 16
CHUNKS = ((3, 5), (0, 3), (5, 8))
DIRS = [(dx, dy) for dx in (-1, 0, 1) for dy in (-1, 0, 1) if (dx, dy) != (0, 0)]


def kernel(
    f_hbm, g_hbm, mask_hbm, list_hbm, w_hbm,
    out_hbm, ig_hbm, wg_hbm,
    mask_ref, list_ref, w_ref, cells, halo_x, halo_y, active, fb, gb, g3, dw, pack, landed, t_sum, r0, relayed, r1, u_sum, r2, v_sum, r3, fin, conv_out,
    in_sem, halo_send, halo_recv, dp_send, dp_recv, s1_send, s1_recv, s2_send, s2_recv, s3_send, s3_recv,
    fin_send, fin_recv, out_sem,
):
    core = lax.axis_index("dp")
    me = lax.axis_index("block")
    chip_z, chip_y, chip_x = me // 16, (me // 4) % 4, me % 4
    block_x, block_y = me // GY, me % GY
    first, second = 1 + 3 * core, 4 - 3 * core
    my_p = chip_x + core * (chip_y - chip_x)
    my_q = chip_y + core * (chip_x - chip_y)

    moves = ((mask_hbm, mask_ref), (list_hbm, list_ref), (f_hbm, cells.at[0]), (g_hbm, cells.at[1]), (w_hbm, w_ref))
    loads = [pltpu.make_async_copy(src, dst, in_sem.at[i]) for i, (src, dst) in enumerate(moves)]
    for load in loads:
        load.start()

    def beside(dx, dy):
        return (core, ((block_x + dx + GX) % GX) * GY + (block_y + dy + GY) % GY)

    def along_p(k):
        return (core, 16 * chip_z + first * ((my_p + k) % 4) + second * my_q)

    def along_q(k):
        return (core, 16 * chip_z + first * my_p + second * ((my_q + k) % 4))

    def along_z(k):
        return (core, 16 * ((chip_z + k) % 8) + me % 16)

    sibling = (1 - core, me)

    barrier = pltpu.get_barrier_semaphore()
    partners = [beside(dx, dy) for dx, dy in DIRS]
    partners += [along_p(k) for k in (1, 2, 3)] + [along_q(k) for k in (1, 2, 3)] + [along_z(k) for k in range(1, 8)]
    partners.append(sibling)
    for partner in partners:
        pl.semaphore_signal(barrier, inc=1, device_id=partner, device_id_type=MESH)
    with jax.named_scope("barrier_wait"):
        pl.semaphore_wait(barrier, len(partners))

    def remote(src, dst, send, recv, device):
        return pltpu.make_async_remote_copy(
            src_ref=src, dst_ref=dst, send_sem=send, recv_sem=recv, device_id=device, device_id_type=MESH
        )

    halos = [{}, {}]
    for i, src in enumerate((cells.at[0], cells.at[1])):
        for n, (dx, dy) in enumerate(DIRS):
            row = LX - 1 if dx == 1 else 0
            col = LY - 1 if dy == 1 else 0
            side_x = 0 if dx == 1 else 1
            side_y = 0 if dy == 1 else 1
            if dx == 0:
                a, b = src.at[:, col], halo_y.at[i, side_y]
            elif dy == 0:
                a, b = src.at[row], halo_x.at[i, side_x, 1:17]
            else:
                a, b = src.at[row, col], halo_x.at[i, side_x, 0 if dy == 1 else 17]
            halos[i][dx, dy] = remote(a, b, halo_send.at[i, n], halo_recv.at[i, n], beside(dx, dy))
    along_y = [d for d in DIRS if d[0] == 0]
    across_x = [d for d in DIRS if d[0] != 0]
    loads[2].wait()
    for d in along_y + across_x:
        halos[0][d].start()

    dw[3456:3464, :] = jnp.zeros((8, C), F32)

    rows_y = lax.broadcasted_iota(jnp.int32, (144, 18), 0) // 8
    pick_y = rows_y == lax.broadcasted_iota(jnp.int32, (144, 18), 1)
    spread = jnp.ones((18, C), BF)
    loads[0].wait()
    loads[1].wait()
    at_z = lax.broadcasted_iota(jnp.int32, (LZ, 18), 0)
    at_y = lax.broadcasted_iota(jnp.int32, (LZ, 18), 1)
    entries = [list_ref[0, n] for n in range(4)]

    def is_listed(brick):
        hit = entries[0] == brick
        for entry in entries[1:]:
            hit = jnp.logical_or(hit, entry == brick)
        return jnp.where(hit, 1, 0)

    def listing_of(half):
        s = [is_listed(4 * half + n) for n in range(4)]
        low = jnp.where(at_z < 4, s[0], s[1])
        high = jnp.where(at_z < 4, s[2], s[3])
        inner = jnp.where(at_y < 9, low, high)
        edge = jnp.logical_or(at_y == 0, at_y == 17)
        return jnp.where(edge, 1, inner)

    halves = [listing_of(0), listing_of(1)]

    def mask_slab(x, listing):
        plane = mask_ref[x, 1:9, 0]
        if listing is not None:
            plane = plane * listing
        by_z = jnp.broadcast_to(plane.astype(F32)[None], (18, LZ, 18)).reshape(144, 18)
        spread_out = jnp.dot(jnp.where(pick_y, by_z, 0.0).astype(BF), spread, preferred_element_type=F32)
        active[x] = spread_out.reshape(18, LZ, C)

    with jax.named_scope("spread_masks"):
        mask_slab(0, None)
        mask_slab(17, None)
        for half in range(2):
            def mask_step(n, carry, half=half):
                mask_slab(1 + 8 * half + n, halves[half])
                return carry
            lax.fori_loop(0, 8, mask_step, 0, unroll=8)

    z_at = lax.broadcasted_iota(jnp.int32, (LY, LZ, C), 1)
    with jax.named_scope("load_wait"):
        for load in loads[3:]:
            load.wait()

    def g3_step(x, carry):
        value = cells[1, x].astype(F32) * active[x + 1, 1:17]
        after = jnp.where(z_at < LZ - 1, pltpu.roll(value, LZ - 1, 1), 0.0)
        before = jnp.where(z_at > 0, pltpu.roll(value, 1, 1), 0.0)
        for c, part in enumerate((after, value, before)):
            g3[x, :, c * C : (c + 1) * C] = part.reshape(128, C).astype(BF)
        return carry

    with jax.named_scope("shift_cotangent"):
        lax.fori_loop(0, LX, g3_step, 0, unroll=2)

    def put(i, dst, x, slab):
        value = slab.astype(F32) * active[x]
        for b in range(3):
            dst[x, :, b * C : (b + 1) * C] = value[b : b + 16].reshape(128, C).astype(BF)

    def columns(i, dst):
        def step(x, carry):
            slab = jnp.concatenate([halo_y[i, 0, pl.ds(x, 1)], cells[i, x], halo_y[i, 1, pl.ds(x, 1)]], axis=0)
            put(i, dst, x + 1, slab)
            return carry

        lax.fori_loop(0, LX, step, 0, unroll=2)

    def margins(i, dst):
        put(i, dst, 0, halo_x[i, 0])
        put(i, dst, 17, halo_x[i, 1])

    def receive(i, dirs):
        for d in dirs:
            halos[i][d].wait_recv()

    with jax.named_scope("wait_halo_y"):
        receive(0, along_y)
    with jax.named_scope("columns_0"):
        columns(0, fb)

    def weight_third(a):
        lhs = fb[a : a + LX].reshape(2048, 3 * C)
        got = lax.dot_general(lhs, g3[...].reshape(2048, 3 * C), (((0,), (0,)), ((), ())), preferred_element_type=F32)
        for b in range(3):
            for c in range(3):
                row = (9 * a + 3 * b + c) * C
                dw[row : row + C, :] = got[b * C : (b + 1) * C, c * C : (c + 1) * C]

    dp_copies = []

    def each_piece(lo, hi, across, start, body):
        p_step, q_step = across

        def plane(z, carry):
            for p in range(4):
                for q in range(4):
                    at = SHARE * 16 * z + (SHARE * p_step * p + SHARE * q_step * q + start)
                    body(z, p, q, dw[pl.ds(at, HALF), :])
            return carry

        lax.fori_loop(lo, hi, plane, 0)

    def send_pair(n):
        lo, hi = CHUNKS[n]

        def body(z, p, q, rows):
            pack[z, p, q] = rows

        each_piece(lo, hi, (second, first), HALF * (1 - core), body)
        copy = remote(pack.at[lo:hi], landed.at[lo:hi], dp_send.at[n], dp_recv.at[n], sibling)
        copy.start()
        dp_copies.append(copy)

    s1_copies, s1_relays, s2_copies = [], [], []
    ahead, behind, across = (my_p + 1) % 4, (my_p + 3) % 4, (my_p + 2) % 4

    def add_pair(n):
        lo, hi = CHUNKS[n]
        with jax.named_scope("wait_pair"):
            dp_copies[n].wait_recv()

        def body(z, p, q, rows):
            t_sum[z, p, q] = rows + landed[z, p, q]

        each_piece(lo, hi, (first, second), HALF * core, body)
        copies = [
            remote(t_sum.at[lo:hi, across, 0:2], r0.at[0, lo:hi], s1_send.at[n, 0], s1_recv.at[n, 0], along_p(1)),
            remote(t_sum.at[lo:hi, across, 2:4], r0.at[1, lo:hi], s1_send.at[n, 1], s1_recv.at[n, 1], along_p(3)),
            remote(t_sum.at[lo:hi, ahead, 2:4], r1.at[0, lo:hi, 2:4], s1_send.at[n, 2], s1_recv.at[n, 2], along_p(1)),
            remote(t_sum.at[lo:hi, behind, 0:2], r1.at[1, lo:hi, 0:2], s1_send.at[n, 3], s1_recv.at[n, 3], along_p(3)),
        ]
        for copy in copies:
            copy.start()
        s1_copies.append(copies)

    def relay(n):
        lo, hi = CHUNKS[n]
        copies = [
            remote(relayed.at[0, lo:hi], r1.at[0, lo:hi, 0:2], s1_send.at[n, 4], s1_recv.at[n, 4], along_p(1)),
            remote(relayed.at[1, lo:hi], r1.at[1, lo:hi, 2:4], s1_send.at[n, 5], s1_recv.at[n, 5], along_p(3)),
        ]
        with jax.named_scope("wait_relay"):
            s1_copies[n][0].wait_recv()
            s1_copies[n][1].wait_recv()
        for z in range(lo, hi):
            relayed[0, z] = t_sum[z, ahead, 0:2] + r0[0, z]
            relayed[1, z] = t_sum[z, behind, 2:4] + r0[1, z]
        for copy in copies:
            copy.start()
        s1_relays.append(copies)

    def add_first(n):
        lo, hi = CHUNKS[n]
        with jax.named_scope("wait_first"):
            for copy in s1_copies[n][2:] + s1_relays[n]:
                copy.wait_recv()
        for z in range(lo, hi):
            u_sum[z] = t_sum[z, my_p] + (r1[0, z] + r1[1, z])
        copies = [
            remote(
                u_sum.at[lo:hi, (my_q + k) % 4], r2.at[k - 1, lo:hi],
                s2_send.at[n, k - 1], s2_recv.at[n, k - 1], along_q(k),
            )
            for k in (1, 2, 3)
        ]
        for copy in copies:
            copy.start()
        s2_copies.append(copies)

    def to_plane(z):
        return remote(v_sum.at[z], r3.at[chip_z], s3_send.at[z], s3_recv.at[chip_z], (core, 16 * z + me % 16))

    def add_second(n):
        lo, hi = CHUNKS[n]
        with jax.named_scope("wait_second"):
            for copy in s2_copies[n]:
                copy.wait_recv()
        for z in range(lo, hi):
            v_sum[z] = (u_sum[z, my_q] + r2[0, z]) + (r2[1, z] + r2[2, z])

            @pl.when(chip_z != z)
            def _():
                to_plane(z).start()

    out_copies = []

    def convolve(i, x0, size):
        src = (fb, gb)[i]
        lhs = jnp.concatenate([src[x0 + a : x0 + a + size].reshape(128 * size, 3 * C) for a in range(3)], axis=1)
        if i == 0:
            rhs = jnp.concatenate(
                [jnp.concatenate([w_ref[3 * ab + c] for c in range(3)], axis=1) for ab in range(9)], axis=0
            )
            acc = jnp.dot(lhs, rhs, preferred_element_type=F32)
        else:
            rhs = jnp.concatenate(
                [jnp.concatenate([w_ref[26 - 3 * ab - c] for ab in range(9)], axis=1) for c in range(3)], axis=0
            )
            acc = lax.dot_general(lhs, rhs, (((1,), (1,)), ((), ())), preferred_element_type=F32)
        acc = acc.reshape(LY * size, LZ, 3 * C)
        z_row = lax.broadcasted_iota(jnp.int32, (LY * size, LZ, C), 1)
        low = jnp.where(z_row > 0, pltpu.roll(acc[:, :, :C], 1, 1), 0.0)
        high = jnp.where(z_row < LZ - 1, pltpu.roll(acc[:, :, 2 * C :], LZ - 1, 1), 0.0)
        inside = active[x0 + 1 : x0 + size + 1, 1:17].reshape(LY * size, LZ, C)
        value = (acc[:, :, C : 2 * C] + low + high) * inside
        conv_out[i, x0 : x0 + size] = value.astype(BF).reshape(size, LY, LZ, C)
        copy = pltpu.make_async_copy(
            conv_out.at[i, x0 : x0 + size], (out_hbm, ig_hbm)[i].at[x0 : x0 + size], out_sem.at[len(out_copies)]
        )
        copy.start()
        out_copies.append(copy)

    for d in DIRS:
        halos[1][d].start()
    with jax.named_scope("weight_third_1"):
        weight_third(1)
    with jax.named_scope("send_pair_0"):
        send_pair(0)
    with jax.named_scope("wait_halo_x"):
        receive(0, across_x)
    margins(0, fb)
    with jax.named_scope("weight_third_0"):
        weight_third(0)
    with jax.named_scope("send_pair_1"):
        send_pair(1)
    with jax.named_scope("add_pair_0"):
        add_pair(0)
    with jax.named_scope("weight_third_2"):
        weight_third(2)
    with jax.named_scope("send_pair_2"):
        send_pair(2)
    with jax.named_scope("add_pair_1"):
        add_pair(1)
    with jax.named_scope("convolve_0_0_4"):
        convolve(0, 0, 4)
    with jax.named_scope("relay_0"):
        relay(0)
    with jax.named_scope("add_pair_2"):
        add_pair(2)
    with jax.named_scope("relay_1"):
        relay(1)
    with jax.named_scope("convolve_0_4_4"):
        convolve(0, 4, 4)
    with jax.named_scope("add_first_0"):
        add_first(0)
    with jax.named_scope("relay_2"):
        relay(2)
    with jax.named_scope("convolve_0_8_4"):
        convolve(0, 8, 4)
    with jax.named_scope("add_first_1"):
        add_first(1)
    with jax.named_scope("add_second_0"):
        add_second(0)
    with jax.named_scope("convolve_0_12_4"):
        convolve(0, 12, 4)
    with jax.named_scope("add_first_2"):
        add_first(2)
    with jax.named_scope("wait_halo_g"):
        receive(1, DIRS)
    with jax.named_scope("columns_1_gb"):
        columns(1, gb)
    with jax.named_scope("margins_1_gb"):
        margins(1, gb)
    with jax.named_scope("convolve_1_0_4"):
        convolve(1, 0, 4)
    with jax.named_scope("add_second_1"):
        add_second(1)
    with jax.named_scope("convolve_1_4_4"):
        convolve(1, 4, 4)
    with jax.named_scope("add_second_2"):
        add_second(2)
    with jax.named_scope("convolve_1_8_8"):
        convolve(1, 8, 8)

    with jax.named_scope("wait_z"):
        for k in range(1, 8):
            z = (chip_z + k) % 8
            remote(v_sum.at[z], r3.at[z], s3_send.at[z], s3_recv.at[z], along_z(k)).wait_recv()
    total = v_sum[chip_z]
    for k in range(1, 8):
        total = total + r3[(chip_z + k) % 8]
    fin[core] = total * (1.0 / math.sqrt(2 * 128 * LX * LY * LZ))
    last = remote(fin.at[core], fin.at[core], fin_send, fin_recv, sibling)
    last.start()
    with jax.named_scope("wait_sends"):
        for copies in [halos[0].values(), halos[1].values()] + s1_copies + s1_relays + s2_copies + [dp_copies]:
            for copy in copies:
                copy.wait_send()
        for k in range(1, 8):
            z = (chip_z + k) % 8
            remote(v_sum.at[z], r3.at[z], s3_send.at[z], s3_recv.at[z], along_z(k)).wait_send()
        for copy in out_copies:
            copy.wait()
    with jax.named_scope("wait_last"):
        last.wait()
    share = pltpu.make_async_copy(fin, wg_hbm, out_sem.at[len(out_copies)])
    share.start()
    share.wait()


def finish(out_in, ig_in, sums_in, out_hbm, ig_hbm, wg_hbm, held, sums, share, in_sem, out_sem):
    first = pltpu.make_async_copy(sums_in, sums, in_sem.at[8])
    first.start()
    parts = [(i, slice(4 * n, 4 * n + 4)) for n in range(4) for i in range(2)]
    loads = [
        pltpu.make_async_copy((out_in, ig_in)[i].at[x], held.at[i, x], in_sem.at[n]) for n, (i, x) in enumerate(parts)
    ]
    stores = [
        pltpu.make_async_copy(held.at[i, x], (out_hbm, ig_hbm)[i].at[x], out_sem.at[n]) for n, (i, x) in enumerate(parts)
    ]
    for load in loads:
        load.start()
    first.wait()
    share[0:HALF, :] = sums[0]
    share[HALF:SHARE, :] = sums[1, 0 : SHARE - HALF]
    last = pltpu.make_async_copy(share, wg_hbm, out_sem.at[8])
    last.start()
    for load, store in zip(loads, stores):
        load.wait()
        store.start()
    for store in stores:
        store.wait()
    last.wait()


def body(features, mask_margin, brick_list, kernel_weight, cotangent):
    hbm = pl.BlockSpec(memory_space=pltpu.HBM)
    vmem = pl.BlockSpec(memory_space=pltpu.VMEM)
    mask = jnp.transpose(mask_margin, (0, 2, 4, 1, 3))[0]
    block = (LX, LY, LZ, C)
    dma = pltpu.SemaphoreType.DMA
    output, input_grad, sums = pl.pallas_call(
        kernel,
        name="conv_and_grads",
        out_shape=(
            jax.ShapeDtypeStruct(block, BF),
            jax.ShapeDtypeStruct(block, BF),
            jax.ShapeDtypeStruct((2, HALF, C), F32),
        ),
        in_specs=[hbm] * 5,
        out_specs=(hbm,) * 3,
        scratch_shapes=[
            pltpu.VMEM((18, 10, 1, 18), jnp.int32),
            pltpu.SMEM((1, 4), jnp.int32),
            pltpu.VMEM((27, C, C), BF),
            pltpu.VMEM((2,) + block, BF),
            pltpu.VMEM((2, 2, 18, LZ, C), BF),
            pltpu.VMEM((2, 2, LX, LZ, C), BF),
            pltpu.VMEM((18, 18, LZ, C), F32),
            pltpu.VMEM((18, 128, 3 * C), BF),
            pltpu.VMEM((18, 128, 3 * C), BF),
            pltpu.VMEM((16, 128, 3 * C), BF),
            pltpu.VMEM((3464, C), F32),
            pltpu.VMEM((8, 4, 4, HALF, C), F32),
            pltpu.VMEM((8, 4, 4, HALF, C), F32),
            pltpu.VMEM((8, 4, 4, HALF, C), F32),
            pltpu.VMEM((2, 8, 2, HALF, C), F32),
            pltpu.VMEM((2, 8, 2, HALF, C), F32),
            pltpu.VMEM((2, 8, 4, HALF, C), F32),
            pltpu.VMEM((8, 4, HALF, C), F32),
            pltpu.VMEM((3, 8, HALF, C), F32),
            pltpu.VMEM((8, HALF, C), F32),
            pltpu.VMEM((8, HALF, C), F32),
            pltpu.VMEM((2, HALF, C), F32),
            pltpu.VMEM((2,) + block, BF),
            dma((5,)),
            dma((2, 8)), dma((2, 8)),
            dma((3,)), dma((3,)),
            dma((3, 6)), dma((3, 6)),
            dma((3, 3)), dma((3, 3)),
            dma((8,)), dma((8,)),
            dma, dma,
            dma((8,)),
        ],
        compiler_params=pltpu.CompilerParams(
            collective_id=0, has_side_effects=True, vmem_limit_bytes=60 * 1024 * 1024
        ),
    )(features[0, 0], cotangent[0, 0], mask, brick_list[0], kernel_weight)
    output, input_grad, share = pl.pallas_call(
        finish,
        name="write_results",
        out_shape=(
            jax.ShapeDtypeStruct(block, BF),
            jax.ShapeDtypeStruct(block, BF),
            jax.ShapeDtypeStruct((SHARE, C), F32),
        ),
        in_specs=[hbm] * 3,
        out_specs=(hbm,) * 3,
        scratch_shapes=[
            pltpu.VMEM((2,) + block, BF),
            pltpu.VMEM((2, HALF, C), F32),
            pltpu.VMEM((SHARE, C), F32),
            dma((9,)),
            dma((9,)),
        ],
        compiler_params=pltpu.CompilerParams(vmem_limit_bytes=60 * 1024 * 1024),
    )(output, input_grad, sums)
    return output[None, None], input_grad[None, None], share.reshape(-1)


def solution(mesh):
    tile = P("dp", "block")
    return jax.shard_map(
        body,
        mesh=mesh,
        in_specs=(tile, tile, tile, P(), tile),
        out_specs=(tile, tile, P("block")),
        check_vma=False,
    )
```

time: 50.4 us -> 40.9 us (0.81)
  local copies, waits for them, and re-layouts: 7 us -> 0 us
  Pallas kernels: 42.5 us -> 40.1 us
    unnamed x11 -> x0, local copies, waits for them, and re-layouts: 6.09 us -> none
    pallas_call x1, Pallas kernels: 42.5 us -> 38 us  [body(): pl.pallas_call(kernel, name='conv_and_grads', out_shape=(jax.ShapeDtypeSt...]
    pallas_call x0 -> x1, Pallas kernels: none -> 2.12 us  [body(): pl.pallas_call(finish, name='write_results', out_shape=(jax.ShapeDtypeStr...]
    squeeze x1 -> x0, local copies, waits for them, and re-layouts: 0.91 us -> none  [body(): mask = jnp.transpose(mask_margin[0, 0], (0, 2, 1))]
where the time goes in v2:
time: 40.9 us; the launch traced here: 40.8 us
  Pallas kernels  40.1 us (98%)
  between operations  0.64 us (2%)
    pallas_call x1, Pallas kernels, body(): pl.pallas_call(kernel, name='conv_and_grads', out_shape=(jax.ShapeDtypeSt...  38 us
    pallas_call x1, Pallas kernels, body(): pl.pallas_call(finish, name='write_results', out_shape=(jax.ShapeDtypeStr...  2.12 us

profile of v2, /device:TPU:1, one launch (start us, length us, event | category | flops | bytes accessed | tf_op | source)
XLA Modules:
  0.0 40.8 jit_solution(8340598873356745892)
XLA Ops:
  0.6 38.0 %conv_and_grads.1 = (bf16[16,16,8,128]{3,2,1,0:T(8,128)(2,1)}, bf16[16,16,8,128]{3,2,1,0:T(8,128)(2,1)}, f32[2,16,128]{2,1,0:T(8,128)}) custom-call(bf16[16,16,8,128]{3,2,1,0:T(8,128)(2,1)} %bitcast.9, bf16[16,16,8,128]{3,2,1,0:T(8,128)(2,1)} %bitcast.10, s32[18,10,1,18]{3,2,1,0:T(1,128)} %bitcast.11, s32[1,4]{1,0:T(1,128)} %bitcast.12, ...), custom_call_target="tpu_custom_call" | custom-call | tf_op jit(solution)/shard_map/conv_and_grads/pallas_call | solution.py:430
  38.6 2.1 %write_results.1 = (bf16[16,16,8,128]{3,2,1,0:T(8,128)(2,1)}, bf16[16,16,8,128]{3,2,1,0:T(8,128)(2,1)}, f32[27,128]{1,0:T(8,128)}) custom-call(bf16[16,16,8,128]{3,2,1,0:T(8,128)(2,1)} %get-tuple-element.9.out_in, bf16[16,16,8,128]{3,2,1,0:T(8,128)(2,1)} %get-tuple-element.10.ig_in, f32[2,16,128]{2,1,0:T(8,128)} %get-tuple-element.11.sums_in), custom_call_target="tpu_custom_call" | custom-call | tf_op jit(solution)/shard_map/write_results/pallas_call | solution.py:477

commit v3 on v2

--- a/solution.py
+++ b/solution.py
@@ -25,7 +25,7 @@
 def kernel(
     f_hbm, g_hbm, mask_hbm, list_hbm, w_hbm,
     out_hbm, ig_hbm, wg_hbm,
-    mask_ref, list_ref, w_ref, cells, halo_x, halo_y, active, fb, gb, g3, dw, pack, landed, t_sum, r0, relayed, r1, u_sum, r2, v_sum, r3, fin, conv_out,
+    mask_ref, list_ref, w_ref, cells, halo_x, halo_y, active, fb, gb, g3, g_edge, dw, pack, landed, t_sum, r1, u_sum, r2, v_sum, r3, fin, conv_out,
     in_sem, halo_send, halo_recv, dp_send, dp_recv, s1_send, s1_recv, s2_send, s2_recv, s3_send, s3_recv,
     fin_send, fin_recv, out_sem,
 ):
@@ -37,11 +37,6 @@
     my_p = chip_x + core * (chip_y - chip_x)
     my_q = chip_y + core * (chip_x - chip_y)
 
-    moves = ((mask_hbm, mask_ref), (list_hbm, list_ref), (f_hbm, cells.at[0]), (g_hbm, cells.at[1]), (w_hbm, w_ref))
-    loads = [pltpu.make_async_copy(src, dst, in_sem.at[i]) for i, (src, dst) in enumerate(moves)]
-    for load in loads:
-        load.start()
-
     def beside(dx, dy):
         return (core, ((block_x + dx + GX) % GX) * GY + (block_y + dy + GY) % GY)
 
@@ -62,9 +57,10 @@
     partners.append(sibling)
     for partner in partners:
         pl.semaphore_signal(barrier, inc=1, device_id=partner, device_id_type=MESH)
-    with jax.named_scope("barrier_wait"):
-        pl.semaphore_wait(barrier, len(partners))
-
+    moves = ((mask_hbm, mask_ref), (list_hbm, list_ref), (f_hbm, cells.at[0]), (g_hbm, cells.at[1]), (w_hbm, w_ref))
+    loads = [pltpu.make_async_copy(src, dst, in_sem.at[i]) for i, (src, dst) in enumerate(moves)]
+    for load in loads:
+        load.start()
     def remote(src, dst, send, recv, device):
         return pltpu.make_async_remote_copy(
             src_ref=src, dst_ref=dst, send_sem=send, recv_sem=recv, device_id=device, device_id_type=MESH
@@ -86,10 +82,6 @@
             halos[i][dx, dy] = remote(a, b, halo_send.at[i, n], halo_recv.at[i, n], beside(dx, dy))
     along_y = [d for d in DIRS if d[0] == 0]
     across_x = [d for d in DIRS if d[0] != 0]
-    loads[2].wait()
-    for d in along_y + across_x:
-        halos[0][d].start()
-
     dw[3456:3464, :] = jnp.zeros((8, C), F32)
 
     rows_y = lax.broadcasted_iota(jnp.int32, (144, 18), 0) // 8
@@ -134,6 +126,12 @@
                 return carry
             lax.fori_loop(0, 8, mask_step, 0, unroll=8)
 
+    with jax.named_scope("barrier_wait"):
+        pl.semaphore_wait(barrier, len(partners))
+    loads[2].wait()
+    for d in along_y + across_x:
+        halos[0][d].start()
+
     z_at = lax.broadcasted_iota(jnp.int32, (LY, LZ, C), 1)
     with jax.named_scope("load_wait"):
         for load in loads[3:]:
@@ -145,6 +143,8 @@
         before = jnp.where(z_at > 0, pltpu.roll(value, 1, 1), 0.0)
         for c, part in enumerate((after, value, before)):
             g3[x, :, c * C : (c + 1) * C] = part.reshape(128, C).astype(BF)
+            g_edge[0, x, :, c * C : (c + 1) * C] = part[0]
+            g_edge[1, x, :, c * C : (c + 1) * C] = part[LY - 1]
         return carry
 
     with jax.named_scope("shift_cotangent"):
@@ -163,6 +163,14 @@
 
         lax.fori_loop(0, LX, step, 0, unroll=2)
 
+    def own_columns():
+        def step(x, carry):
+            none = jnp.zeros((1, LZ, C), BF)
+            put(0, fb, x + 1, jnp.concatenate([none, cells[0, x], none], axis=0))
+            return carry
+
+        lax.fori_loop(0, LX, step, 0, unroll=2)
+
     def margins(i, dst):
         put(i, dst, 0, halo_x[i, 0])
         put(i, dst, 17, halo_x[i, 1])
@@ -171,18 +179,43 @@
         for d in dirs:
             halos[i][d].wait_recv()
 
-    with jax.named_scope("wait_halo_y"):
-        receive(0, along_y)
-    with jax.named_scope("columns_0"):
-        columns(0, fb)
+    with jax.named_scope("own_columns"):
+        own_columns()
+
+    def by_rows(lhs, rhs):
+        return lax.dot_general(lhs, rhs, (((0,), (0,)), ((), ())), preferred_element_type=F32)
+
+    def place(a, b, got, add):
+        for c in range(3):
+            row = (9 * a + 3 * b + c) * C
+            part = got[:, c * C : (c + 1) * C]
+            dw[row : row + C, :] = dw[row : row + C, :] + part if add else part
 
     def weight_third(a):
-        lhs = fb[a : a + LX].reshape(2048, 3 * C)
-        got = lax.dot_general(lhs, g3[...].reshape(2048, 3 * C), (((0,), (0,)), ((), ())), preferred_element_type=F32)
+        lo, hi = max(0, 1 - a), min(LX, LX + 1 - a)
+        rows = 128 * (hi - lo)
+        got = by_rows(fb[a + lo : a + hi].reshape(rows, 3 * C), g3[lo:hi].reshape(rows, 3 * C))
         for b in range(3):
-            for c in range(3):
-                row = (9 * a + 3 * b + c) * C
-                dw[row : row + C, :] = got[b * C : (b + 1) * C, c * C : (c + 1) * C]
+            place(a, b, got[b * C : (b + 1) * C], a == 2 and b != 1)
+
+    def weight_y():
+        none = jnp.zeros((1, LZ, C), F32)
+        for side, b in ((0, 0), (1, 2)):
+            edge = halo_y[0, side].astype(F32) * active[1:17, 17 * side]
+            shifted = [
+                jnp.concatenate([none, edge[: LX - 1]], axis=0),
+                edge,
+                jnp.concatenate([edge[1:], none], axis=0),
+            ]
+            lhs = jnp.concatenate([part.reshape(128, C).astype(BF) for part in shifted], axis=1)
+            got = by_rows(lhs, g_edge[side].reshape(128, 3 * C).astype(BF))
+            for a in range(3):
+                place(a, b, got[a * C : (a + 1) * C], a != 2)
+
+    def weight_x(a):
+        got = by_rows(fb[0 if a == 0 else LX + 1], g3[0 if a == 0 else LX - 1])
+        for b in range(3):
+            place(a, b, got[b * C : (b + 1) * C], True)
 
     dp_copies = []
 
@@ -209,8 +242,7 @@
         copy.start()
         dp_copies.append(copy)
 
-    s1_copies, s1_relays, s2_copies = [], [], []
-    ahead, behind, across = (my_p + 1) % 4, (my_p + 3) % 4, (my_p + 2) % 4
+    s1_copies, s2_copies = [], []
 
     def add_pair(n):
         lo, hi = CHUNKS[n]
@@ -222,38 +254,23 @@
 
         each_piece(lo, hi, (first, second), HALF * core, body)
         copies = [
-            remote(t_sum.at[lo:hi, across, 0:2], r0.at[0, lo:hi], s1_send.at[n, 0], s1_recv.at[n, 0], along_p(1)),
-            remote(t_sum.at[lo:hi, across, 2:4], r0.at[1, lo:hi], s1_send.at[n, 1], s1_recv.at[n, 1], along_p(3)),
-            remote(t_sum.at[lo:hi, ahead, 2:4], r1.at[0, lo:hi, 2:4], s1_send.at[n, 2], s1_recv.at[n, 2], along_p(1)),
-            remote(t_sum.at[lo:hi, behind, 0:2], r1.at[1, lo:hi, 0:2], s1_send.at[n, 3], s1_recv.at[n, 3], along_p(3)),
+            remote(
+                t_sum.at[lo:hi, (my_p + k) % 4], r1.at[k - 1, lo:hi],
+                s1_send.at[n, k - 1], s1_recv.at[n, k - 1], along_p(k),
+            )
+            for k in (1, 2, 3)
         ]
         for copy in copies:
             copy.start()
         s1_copies.append(copies)
 
-    def relay(n):
-        lo, hi = CHUNKS[n]
-        copies = [
-            remote(relayed.at[0, lo:hi], r1.at[0, lo:hi, 0:2], s1_send.at[n, 4], s1_recv.at[n, 4], along_p(1)),
-            remote(relayed.at[1, lo:hi], r1.at[1, lo:hi, 2:4], s1_send.at[n, 5], s1_recv.at[n, 5], along_p(3)),
-        ]
-        with jax.named_scope("wait_relay"):
-            s1_copies[n][0].wait_recv()
-            s1_copies[n][1].wait_recv()
-        for z in range(lo, hi):
-            relayed[0, z] = t_sum[z, ahead, 0:2] + r0[0, z]
-            relayed[1, z] = t_sum[z, behind, 2:4] + r0[1, z]
-        for copy in copies:
-            copy.start()
-        s1_relays.append(copies)
-
     def add_first(n):
         lo, hi = CHUNKS[n]
         with jax.named_scope("wait_first"):
-            for copy in s1_copies[n][2:] + s1_relays[n]:
+            for copy in s1_copies[n]:
                 copy.wait_recv()
         for z in range(lo, hi):
-            u_sum[z] = t_sum[z, my_p] + (r1[0, z] + r1[1, z])
+            u_sum[z] = (t_sum[z, my_p] + r1[0, z]) + (r1[1, z] + r1[2, z])
         copies = [
             remote(
                 u_sum.at[lo:hi, (my_q + k) % 4], r2.at[k - 1, lo:hi],
@@ -308,47 +325,49 @@
         copy.start()
         out_copies.append(copy)
 
+    with jax.named_scope("weight_third_1"):
+        weight_third(1)
     for d in DIRS:
         halos[1][d].start()
-    with jax.named_scope("weight_third_1"):
-        weight_third(1)
+    with jax.named_scope("weight_third_0"):
+        weight_third(0)
+    with jax.named_scope("wait_halo_y"):
+        receive(0, along_y)
+    with jax.named_scope("weight_y_"):
+        weight_y()
     with jax.named_scope("send_pair_0"):
         send_pair(0)
+    with jax.named_scope("weight_third_2"):
+        weight_third(2)
+    with jax.named_scope("add_pair_0"):
+        add_pair(0)
     with jax.named_scope("wait_halo_x"):
         receive(0, across_x)
     margins(0, fb)
-    with jax.named_scope("weight_third_0"):
-        weight_third(0)
+    with jax.named_scope("weight_x_0"):
+        weight_x(0)
     with jax.named_scope("send_pair_1"):
         send_pair(1)
-    with jax.named_scope("add_pair_0"):
-        add_pair(0)
-    with jax.named_scope("weight_third_2"):
-        weight_third(2)
+    with jax.named_scope("weight_x_2"):
+        weight_x(2)
     with jax.named_scope("send_pair_2"):
         send_pair(2)
+    with jax.named_scope("columns_0_fb"):
+        columns(0, fb)
     with jax.named_scope("add_pair_1"):
         add_pair(1)
+    with jax.named_scope("add_pair_2"):
+        add_pair(2)
     with jax.named_scope("convolve_0_0_4"):
         convolve(0, 0, 4)
-    with jax.named_scope("relay_0"):
-        relay(0)
-    with jax.named_scope("add_pair_2"):
-        add_pair(2)
-    with jax.named_scope("relay_1"):
-        relay(1)
     with jax.named_scope("convolve_0_4_4"):
         convolve(0, 4, 4)
     with jax.named_scope("add_first_0"):
         add_first(0)
-    with jax.named_scope("relay_2"):
-        relay(2)
+    with jax.named_scope("add_first_1"):
+        add_first(1)
     with jax.named_scope("convolve_0_8_4"):
         convolve(0, 8, 4)
-    with jax.named_scope("add_first_1"):
-        add_first(1)
-    with jax.named_scope("add_second_0"):
-        add_second(0)
     with jax.named_scope("convolve_0_12_4"):
         convolve(0, 12, 4)
     with jax.named_scope("add_first_2"):
@@ -361,15 +380,18 @@
         margins(1, gb)
     with jax.named_scope("convolve_1_0_4"):
         convolve(1, 0, 4)
+    with jax.named_scope("add_second_0"):
+        add_second(0)
     with jax.named_scope("add_second_1"):
         add_second(1)
     with jax.named_scope("convolve_1_4_4"):
         convolve(1, 4, 4)
     with jax.named_scope("add_second_2"):
         add_second(2)
-    with jax.named_scope("convolve_1_8_8"):
-        convolve(1, 8, 8)
-
+    with jax.named_scope("convolve_1_8_4"):
+        convolve(1, 8, 4)
+    with jax.named_scope("convolve_1_12_4"):
+        convolve(1, 12, 4)
     with jax.named_scope("wait_z"):
         for k in range(1, 8):
             z = (chip_z + k) % 8
@@ -377,11 +399,13 @@
     total = v_sum[chip_z]
     for k in range(1, 8):
         total = total + r3[(chip_z + k) % 8]
-    fin[core] = total * (1.0 / math.sqrt(2 * 128 * LX * LY * LZ))
-    last = remote(fin.at[core], fin.at[core], fin_send, fin_recv, sibling)
+    fin[...] = total * (1.0 / math.sqrt(2 * 128 * LX * LY * LZ))
+    last = remote(fin, wg_hbm.at[core], fin_send, fin_recv, sibling)
     last.start()
+    own = pltpu.make_async_copy(fin, wg_hbm.at[core], out_sem.at[8])
+    own.start()
     with jax.named_scope("wait_sends"):
-        for copies in [halos[0].values(), halos[1].values()] + s1_copies + s1_relays + s2_copies + [dp_copies]:
+        for copies in [halos[0].values(), halos[1].values()] + s1_copies + s2_copies + [dp_copies]:
             for copy in copies:
                 copy.wait_send()
         for k in range(1, 8):
@@ -389,11 +413,9 @@
             remote(v_sum.at[z], r3.at[z], s3_send.at[z], s3_recv.at[z], along_z(k)).wait_send()
         for copy in out_copies:
             copy.wait()
+        own.wait()
     with jax.named_scope("wait_last"):
         last.wait()
-    share = pltpu.make_async_copy(fin, wg_hbm, out_sem.at[len(out_copies)])
-    share.start()
-    share.wait()
 
 
 def finish(out_in, ig_in, sums_in, out_hbm, ig_hbm, wg_hbm, held, sums, share, in_sem, out_sem):
@@ -448,27 +470,26 @@
             pltpu.VMEM((18, 128, 3 * C), BF),
             pltpu.VMEM((18, 128, 3 * C), BF),
             pltpu.VMEM((16, 128, 3 * C), BF),
+            pltpu.VMEM((2, 16, LZ, 3 * C), F32),
             pltpu.VMEM((3464, C), F32),
             pltpu.VMEM((8, 4, 4, HALF, C), F32),
             pltpu.VMEM((8, 4, 4, HALF, C), F32),
             pltpu.VMEM((8, 4, 4, HALF, C), F32),
-            pltpu.VMEM((2, 8, 2, HALF, C), F32),
-            pltpu.VMEM((2, 8, 2, HALF, C), F32),
-            pltpu.VMEM((2, 8, 4, HALF, C), F32),
+            pltpu.VMEM((3, 8, 4, HALF, C), F32),
             pltpu.VMEM((8, 4, HALF, C), F32),
             pltpu.VMEM((3, 8, HALF, C), F32),
             pltpu.VMEM((8, HALF, C), F32),
             pltpu.VMEM((8, HALF, C), F32),
-            pltpu.VMEM((2, HALF, C), F32),
+            pltpu.VMEM((HALF, C), F32),
             pltpu.VMEM((2,) + block, BF),
             dma((5,)),
             dma((2, 8)), dma((2, 8)),
             dma((3,)), dma((3,)),
-            dma((3, 6)), dma((3, 6)),
+            dma((3, 3)), dma((3, 3)),
             dma((3, 3)), dma((3, 3)),
             dma((8,)), dma((8,)),
             dma, dma,
-            dma((8,)),
+            dma((9,)),
         ],
         compiler_params=pltpu.CompilerParams(
             collective_id=0, has_side_effects=True, vmem_limit_bytes=60 * 1024 * 1024

time: 40.9 us -> 37.5 us (0.917)
  Pallas kernels: 40.1 us -> 36.6 us
    pallas_call x1, Pallas kernels: 38 us -> 34.5 us  [body(): pl.pallas_call(kernel, name='conv_and_grads', out_shape=(jax.ShapeDtypeSt...]
where the time goes in v3:
time: 37.5 us; the launch traced here: 37.3 us
  Pallas kernels  36.6 us (98%)
  between operations  0.64 us (2%)
    pallas_call x1, Pallas kernels, body(): pl.pallas_call(kernel, name='conv_and_grads', out_shape=(jax.ShapeDtypeSt...  34.5 us
    pallas_call x1, Pallas kernels, body(): pl.pallas_call(finish, name='write_results', out_shape=(jax.ShapeDtypeStr...  2.12 us

profile of v3, /device:TPU:1, one launch (start us, length us, event | category | flops | bytes accessed | tf_op | source)
XLA Modules:
  0.0 37.3 jit_solution(15636819929584831742)
XLA Ops:
  0.6 34.5 %conv_and_grads.1 = (bf16[16,16,8,128]{3,2,1,0:T(8,128)(2,1)}, bf16[16,16,8,128]{3,2,1,0:T(8,128)(2,1)}, f32[2,16,128]{2,1,0:T(8,128)}) custom-call(bf16[16,16,8,128]{3,2,1,0:T(8,128)(2,1)} %bitcast.9, bf16[16,16,8,128]{3,2,1,0:T(8,128)(2,1)} %bitcast.10, s32[18,10,1,18]{3,2,1,0:T(1,128)} %bitcast.11, s32[1,4]{1,0:T(1,128)} %bitcast.12, ...), custom_call_target="tpu_custom_call" | custom-call | tf_op jit(solution)/shard_map/conv_and_grads/pallas_call | solution.py:452
  35.2 2.1 %write_results.1 = (bf16[16,16,8,128]{3,2,1,0:T(8,128)(2,1)}, bf16[16,16,8,128]{3,2,1,0:T(8,128)(2,1)}, f32[27,128]{1,0:T(8,128)}) custom-call(bf16[16,16,8,128]{3,2,1,0:T(8,128)(2,1)} %get-tuple-element.9.out_in, bf16[16,16,8,128]{3,2,1,0:T(8,128)(2,1)} %get-tuple-element.10.ig_in, f32[2,16,128]{2,1,0:T(8,128)} %get-tuple-element.11.sums_in), custom_call_target="tpu_custom_call" | custom-call | tf_op jit(solution)/shard_map/write_results/pallas_call | solution.py:498

commit v4 on v3

--- a/solution.py
+++ b/solution.py
@@ -27,7 +27,7 @@
     out_hbm, ig_hbm, wg_hbm,
     mask_ref, list_ref, w_ref, cells, halo_x, halo_y, active, fb, gb, g3, g_edge, dw, pack, landed, t_sum, r1, u_sum, r2, v_sum, r3, fin, conv_out,
     in_sem, halo_send, halo_recv, dp_send, dp_recv, s1_send, s1_recv, s2_send, s2_recv, s3_send, s3_recv,
-    fin_send, fin_recv, out_sem,
+    out_sem,
 ):
     core = lax.axis_index("dp")
     me = lax.axis_index("block")
@@ -54,7 +54,7 @@
     barrier = pltpu.get_barrier_semaphore()
     partners = [beside(dx, dy) for dx, dy in DIRS]
     partners += [along_p(k) for k in (1, 2, 3)] + [along_q(k) for k in (1, 2, 3)] + [along_z(k) for k in range(1, 8)]
-    partners.append(sibling)
+    partners += [(1 - core, 16 * ((chip_z + k) % 8) + me % 16) for k in range(8)]
     for partner in partners:
         pl.semaphore_signal(barrier, inc=1, device_id=partner, device_id_type=MESH)
     moves = ((mask_hbm, mask_ref), (list_hbm, list_ref), (f_hbm, cells.at[0]), (g_hbm, cells.at[1]), (w_hbm, w_ref))
@@ -66,9 +66,12 @@
             src_ref=src, dst_ref=dst, send_sem=send, recv_sem=recv, device_id=device, device_id_type=MESH
         )
 
+    def drain(sem, like):
+        pltpu.make_async_copy(like, like, sem).wait()
+
     halos = [{}, {}]
     for i, src in enumerate((cells.at[0], cells.at[1])):
-        for n, (dx, dy) in enumerate(DIRS):
+        for dx, dy in DIRS:
             row = LX - 1 if dx == 1 else 0
             col = LY - 1 if dy == 1 else 0
             side_x = 0 if dx == 1 else 1
@@ -79,9 +82,15 @@
                 a, b = src.at[row], halo_x.at[i, side_x, 1:17]
             else:
                 a, b = src.at[row, col], halo_x.at[i, side_x, 0 if dy == 1 else 17]
-            halos[i][dx, dy] = remote(a, b, halo_send.at[i, n], halo_recv.at[i, n], beside(dx, dy))
+            halos[i][dx, dy] = remote(a, b, halo_send.at[min(abs(dx), 1)], halo_recv.at[i, min(abs(dx), 1)], beside(dx, dy))
     along_y = [d for d in DIRS if d[0] == 0]
     across_x = [d for d in DIRS if d[0] != 0]
+    with jax.named_scope("barrier_wait"):
+        pl.semaphore_wait(barrier, len(partners))
+    loads[2].wait()
+    for d in along_y + across_x:
+        halos[0][d].start()
+
     dw[3456:3464, :] = jnp.zeros((8, C), F32)
 
     rows_y = lax.broadcasted_iota(jnp.int32, (144, 18), 0) // 8
@@ -125,12 +134,6 @@
                 mask_slab(1 + 8 * half + n, halves[half])
                 return carry
             lax.fori_loop(0, 8, mask_step, 0, unroll=8)
-
-    with jax.named_scope("barrier_wait"):
-        pl.semaphore_wait(barrier, len(partners))
-    loads[2].wait()
-    for d in along_y + across_x:
-        halos[0][d].start()
 
     z_at = lax.broadcasted_iota(jnp.int32, (LY, LZ, C), 1)
     with jax.named_scope("load_wait"):
@@ -174,10 +177,6 @@
     def margins(i, dst):
         put(i, dst, 0, halo_x[i, 0])
         put(i, dst, 17, halo_x[i, 1])
-
-    def receive(i, dirs):
-        for d in dirs:
-            halos[i][d].wait_recv()
 
     with jax.named_scope("own_columns"):
         own_columns()
@@ -217,8 +216,6 @@
         for b in range(3):
             place(a, b, got[b * C : (b + 1) * C], True)
 
-    dp_copies = []
-
     def each_piece(lo, hi, across, start, body):
         p_step, q_step = across
 
@@ -238,16 +235,13 @@
             pack[z, p, q] = rows
 
         each_piece(lo, hi, (second, first), HALF * (1 - core), body)
-        copy = remote(pack.at[lo:hi], landed.at[lo:hi], dp_send.at[n], dp_recv.at[n], sibling)
+        copy = remote(pack.at[lo:hi], landed.at[lo:hi], dp_send, dp_recv.at[n], sibling)
         copy.start()
-        dp_copies.append(copy)
-
-    s1_copies, s2_copies = [], []
 
     def add_pair(n):
         lo, hi = CHUNKS[n]
         with jax.named_scope("wait_pair"):
-            dp_copies[n].wait_recv()
+            drain(dp_recv.at[n], landed.at[lo:hi])
 
         def body(z, p, q, rows):
             t_sum[z, p, q] = rows + landed[z, p, q]
@@ -256,48 +250,45 @@
         copies = [
             remote(
                 t_sum.at[lo:hi, (my_p + k) % 4], r1.at[k - 1, lo:hi],
-                s1_send.at[n, k - 1], s1_recv.at[n, k - 1], along_p(k),
+                s1_send, s1_recv.at[n], along_p(k),
             )
             for k in (1, 2, 3)
         ]
         for copy in copies:
             copy.start()
-        s1_copies.append(copies)
 
     def add_first(n):
         lo, hi = CHUNKS[n]
         with jax.named_scope("wait_first"):
-            for copy in s1_copies[n]:
-                copy.wait_recv()
+            drain(s1_recv.at[n], r1.at[:, lo:hi])
         for z in range(lo, hi):
             u_sum[z] = (t_sum[z, my_p] + r1[0, z]) + (r1[1, z] + r1[2, z])
         copies = [
             remote(
                 u_sum.at[lo:hi, (my_q + k) % 4], r2.at[k - 1, lo:hi],
-                s2_send.at[n, k - 1], s2_recv.at[n, k - 1], along_q(k),
+                s2_send, s2_recv.at[n], along_q(k),
             )
             for k in (1, 2, 3)
         ]
         for copy in copies:
             copy.start()
-        s2_copies.append(copies)
-
-    def to_plane(z):
-        return remote(v_sum.at[z], r3.at[chip_z], s3_send.at[z], s3_recv.at[chip_z], (core, 16 * z + me % 16))
+
+    def to_share(z, side):
+        recv = s3_recv.at[0 if side is core else 1]
+        return remote(v_sum.at[z], r3.at[core, chip_z], s3_send, recv, (side, 16 * z + me % 16))
 
     def add_second(n):
         lo, hi = CHUNKS[n]
         with jax.named_scope("wait_second"):
-            for copy in s2_copies[n]:
-                copy.wait_recv()
+            drain(s2_recv.at[n], r2.at[:, lo:hi])
         for z in range(lo, hi):
             v_sum[z] = (u_sum[z, my_q] + r2[0, z]) + (r2[1, z] + r2[2, z])
 
             @pl.when(chip_z != z)
             def _():
-                to_plane(z).start()
-
-    out_copies = []
+                to_share(z, core).start()
+
+            to_share(z, 1 - core).start()
 
     def convolve(i, x0, size):
         src = (fb, gb)[i]
@@ -320,10 +311,9 @@
         value = (acc[:, :, C : 2 * C] + low + high) * inside
         conv_out[i, x0 : x0 + size] = value.astype(BF).reshape(size, LY, LZ, C)
         copy = pltpu.make_async_copy(
-            conv_out.at[i, x0 : x0 + size], (out_hbm, ig_hbm)[i].at[x0 : x0 + size], out_sem.at[len(out_copies)]
+            conv_out.at[i, x0 : x0 + size], (out_hbm, ig_hbm)[i].at[x0 : x0 + size], out_sem.at[0]
         )
         copy.start()
-        out_copies.append(copy)
 
     with jax.named_scope("weight_third_1"):
         weight_third(1)
@@ -332,22 +322,22 @@
     with jax.named_scope("weight_third_0"):
         weight_third(0)
     with jax.named_scope("wait_halo_y"):
-        receive(0, along_y)
+        drain(halo_recv.at[0, 0], halo_y.at[0])
     with jax.named_scope("weight_y_"):
         weight_y()
     with jax.named_scope("send_pair_0"):
         send_pair(0)
     with jax.named_scope("weight_third_2"):
         weight_third(2)
-    with jax.named_scope("add_pair_0"):
-        add_pair(0)
     with jax.named_scope("wait_halo_x"):
-        receive(0, across_x)
+        drain(halo_recv.at[0, 1], halo_x.at[0])
     margins(0, fb)
     with jax.named_scope("weight_x_0"):
         weight_x(0)
     with jax.named_scope("send_pair_1"):
         send_pair(1)
+    with jax.named_scope("add_pair_0"):
+        add_pair(0)
     with jax.named_scope("weight_x_2"):
         weight_x(2)
     with jax.named_scope("send_pair_2"):
@@ -364,16 +354,17 @@
         convolve(0, 4, 4)
     with jax.named_scope("add_first_0"):
         add_first(0)
+    with jax.named_scope("convolve_0_8_4"):
+        convolve(0, 8, 4)
     with jax.named_scope("add_first_1"):
         add_first(1)
-    with jax.named_scope("convolve_0_8_4"):
-        convolve(0, 8, 4)
     with jax.named_scope("convolve_0_12_4"):
         convolve(0, 12, 4)
     with jax.named_scope("add_first_2"):
         add_first(2)
     with jax.named_scope("wait_halo_g"):
-        receive(1, DIRS)
+        drain(halo_recv.at[1, 0], halo_y.at[1])
+        drain(halo_recv.at[1, 1], halo_x.at[1])
     with jax.named_scope("columns_1_gb"):
         columns(1, gb)
     with jax.named_scope("margins_1_gb"):
@@ -392,30 +383,26 @@
         convolve(1, 8, 4)
     with jax.named_scope("convolve_1_12_4"):
         convolve(1, 12, 4)
+    r3[core, chip_z] = v_sum[chip_z]
     with jax.named_scope("wait_z"):
-        for k in range(1, 8):
-            z = (chip_z + k) % 8
-            remote(v_sum.at[z], r3.at[z], s3_send.at[z], s3_recv.at[z], along_z(k)).wait_recv()
-    total = v_sum[chip_z]
-    for k in range(1, 8):
-        total = total + r3[(chip_z + k) % 8]
-    fin[...] = total * (1.0 / math.sqrt(2 * 128 * LX * LY * LZ))
-    last = remote(fin, wg_hbm.at[core], fin_send, fin_recv, sibling)
-    last.start()
-    own = pltpu.make_async_copy(fin, wg_hbm.at[core], out_sem.at[8])
+        drain(s3_recv.at[0], r3.at[0, 0:7])
+        drain(s3_recv.at[1], r3.at[1])
+    for half in range(2):
+        terms = [r3[half, z] for z in range(8)]
+        while len(terms) > 1:
+            terms = [a + b for a, b in zip(terms[::2], terms[1::2])]
+        fin[half] = terms[0] * (1.0 / math.sqrt(2 * 128 * LX * LY * LZ))
+    own = pltpu.make_async_copy(fin, wg_hbm, out_sem.at[1])
     own.start()
     with jax.named_scope("wait_sends"):
-        for copies in [halos[0].values(), halos[1].values()] + s1_copies + s2_copies + [dp_copies]:
-            for copy in copies:
-                copy.wait_send()
-        for k in range(1, 8):
-            z = (chip_z + k) % 8
-            remote(v_sum.at[z], r3.at[z], s3_send.at[z], s3_recv.at[z], along_z(k)).wait_send()
-        for copy in out_copies:
-            copy.wait()
+        drain(halo_send.at[0], halo_y)
+        drain(halo_send.at[1], halo_x)
+        drain(dp_send, pack)
+        drain(s1_send, r1)
+        drain(s2_send, r2)
+        drain(s3_send, r2.at[:, 0:5])
+        drain(out_sem.at[0], conv_out)
         own.wait()
-    with jax.named_scope("wait_last"):
-        last.wait()
 
 
 def finish(out_in, ig_in, sums_in, out_hbm, ig_hbm, wg_hbm, held, sums, share, in_sem, out_sem):
@@ -479,17 +466,16 @@
             pltpu.VMEM((8, 4, HALF, C), F32),
             pltpu.VMEM((3, 8, HALF, C), F32),
             pltpu.VMEM((8, HALF, C), F32),
-            pltpu.VMEM((8, HALF, C), F32),
-            pltpu.VMEM((HALF, C), F32),
+            pltpu.VMEM((2, 8, HALF, C), F32),
+            pltpu.VMEM((2, HALF, C), F32),
             pltpu.VMEM((2,) + block, BF),
             dma((5,)),
-            dma((2, 8)), dma((2, 8)),
-            dma((3,)), dma((3,)),
-            dma((3, 3)), dma((3, 3)),
-            dma((3, 3)), dma((3, 3)),
-            dma((8,)), dma((8,)),
-            dma, dma,
-            dma((9,)),
+            dma((2,)), dma((2, 2)),
+            dma, dma((3,)),
+            dma, dma((3,)),
+            dma, dma((3,)),
+            dma, dma((2,)),
+            dma((2,)),
         ],
         compiler_params=pltpu.CompilerParams(
             collective_id=0, has_side_effects=True, vmem_limit_bytes=60 * 1024 * 1024

time: 37.5 us -> 36.2 us (0.965)
  Pallas kernels: 36.6 us -> 35.4 us
    pallas_call x1, Pallas kernels: 34.5 us -> 33.3 us  [body(): pl.pallas_call(kernel, name='conv_and_grads', out_shape=(jax.ShapeDtypeSt...]
where the time goes in v4:
time: 36.2 us; the launch traced here: 36.1 us
  Pallas kernels  35.4 us (98%)
  between operations  0.64 us (2%)
    pallas_call x1, Pallas kernels, body(): pl.pallas_call(kernel, name='conv_and_grads', out_shape=(jax.ShapeDtypeSt...  33.3 us
    pallas_call x1, Pallas kernels, body(): pl.pallas_call(finish, name='write_results', out_shape=(jax.ShapeDtypeStr...  2.12 us

profile of v4, /device:TPU:1, one launch (start us, length us, event | category | flops | bytes accessed | tf_op | source)
XLA Modules:
  0.0 36.1 jit_solution(487787532994581614)
XLA Ops:
  0.6 33.3 %conv_and_grads.1 = (bf16[16,16,8,128]{3,2,1,0:T(8,128)(2,1)}, bf16[16,16,8,128]{3,2,1,0:T(8,128)(2,1)}, f32[2,16,128]{2,1,0:T(8,128)}) custom-call(bf16[16,16,8,128]{3,2,1,0:T(8,128)(2,1)} %bitcast.9, bf16[16,16,8,128]{3,2,1,0:T(8,128)(2,1)} %bitcast.10, s32[18,10,1,18]{3,2,1,0:T(1,128)} %bitcast.11, s32[1,4]{1,0:T(1,128)} %bitcast.12, ...), custom_call_target="tpu_custom_call" | custom-call | tf_op jit(solution)/shard_map/conv_and_grads/pallas_call | solution.py:439
  33.9 2.1 %write_results.1 = (bf16[16,16,8,128]{3,2,1,0:T(8,128)(2,1)}, bf16[16,16,8,128]{3,2,1,0:T(8,128)(2,1)}, f32[27,128]{1,0:T(8,128)}) custom-call(bf16[16,16,8,128]{3,2,1,0:T(8,128)(2,1)} %get-tuple-element.9.out_in, bf16[16,16,8,128]{3,2,1,0:T(8,128)(2,1)} %get-tuple-element.10.ig_in, f32[2,16,128]{2,1,0:T(8,128)} %get-tuple-element.11.sums_in), custom_call_target="tpu_custom_call" | custom-call | tf_op jit(solution)/shard_map/write_results/pallas_call | solution.py:484

commit v5 on v4

--- a/solution.py
+++ b/solution.py
@@ -33,17 +33,20 @@
     me = lax.axis_index("block")
     chip_z, chip_y, chip_x = me // 16, (me // 4) % 4, me % 4
     block_x, block_y = me // GY, me % GY
-    first, second = 1 + 3 * core, 4 - 3 * core
-    my_p = chip_x + core * (chip_y - chip_x)
-    my_q = chip_y + core * (chip_x - chip_y)
+    def roles(n, which):
+        turned = 1 if n == 0 else which
+        first, second = 1 + 3 * turned, 4 - 3 * turned
+        return first, second, chip_x + turned * (chip_y - chip_x), chip_y + turned * (chip_x - chip_y)
 
     def beside(dx, dy):
         return (core, ((block_x + dx + GX) % GX) * GY + (block_y + dy + GY) % GY)
 
-    def along_p(k):
+    def along_p(n, k):
+        first, second, my_p, my_q = roles(n, core)
         return (core, 16 * chip_z + first * ((my_p + k) % 4) + second * my_q)
 
-    def along_q(k):
+    def along_q(n, k):
+        first, second, my_p, my_q = roles(n, core)
         return (core, 16 * chip_z + first * my_p + second * ((my_q + k) % 4))
 
     def along_z(k):
@@ -53,7 +56,7 @@
 
     barrier = pltpu.get_barrier_semaphore()
     partners = [beside(dx, dy) for dx, dy in DIRS]
-    partners += [along_p(k) for k in (1, 2, 3)] + [along_q(k) for k in (1, 2, 3)] + [along_z(k) for k in range(1, 8)]
+    partners += [along_p(2, k) for k in (1, 2, 3)] + [along_q(2, k) for k in (1, 2, 3)] + [along_z(k) for k in range(1, 8)]
     partners += [(1 - core, 16 * ((chip_z + k) % 8) + me % 16) for k in range(8)]
     for partner in partners:
         pl.semaphore_signal(barrier, inc=1, device_id=partner, device_id_type=MESH)
@@ -234,7 +237,7 @@
         def body(z, p, q, rows):
             pack[z, p, q] = rows
 
-        each_piece(lo, hi, (second, first), HALF * (1 - core), body)
+        each_piece(lo, hi, roles(n, 1 - core)[:2], HALF * (1 - core), body)
         copy = remote(pack.at[lo:hi], landed.at[lo:hi], dp_send, dp_recv.at[n], sibling)
         copy.start()
 
@@ -246,11 +249,12 @@
         def body(z, p, q, rows):
             t_sum[z, p, q] = rows + landed[z, p, q]
 
+        first, second, my_p, my_q = roles(n, core)
         each_piece(lo, hi, (first, second), HALF * core, body)
         copies = [
             remote(
                 t_sum.at[lo:hi, (my_p + k) % 4], r1.at[k - 1, lo:hi],
-                s1_send, s1_recv.at[n], along_p(k),
+                s1_send, s1_recv.at[n], along_p(n, k),
             )
             for k in (1, 2, 3)
         ]
@@ -259,6 +263,7 @@
 
     def add_first(n):
         lo, hi = CHUNKS[n]
+        first, second, my_p, my_q = roles(n, core)
         with jax.named_scope("wait_first"):
             drain(s1_recv.at[n], r1.at[:, lo:hi])
         for z in range(lo, hi):
@@ -266,7 +271,7 @@
         copies = [
             remote(
                 u_sum.at[lo:hi, (my_q + k) % 4], r2.at[k - 1, lo:hi],
-                s2_send, s2_recv.at[n], along_q(k),
+                s2_send, s2_recv.at[n], along_q(n, k),
             )
             for k in (1, 2, 3)
         ]
@@ -279,6 +284,7 @@
 
     def add_second(n):
         lo, hi = CHUNKS[n]
+        my_q = roles(n, core)[3]
         with jax.named_scope("wait_second"):
             drain(s2_recv.at[n], r2.at[:, lo:hi])
         for z in range(lo, hi):
@@ -406,9 +412,9 @@
 
 
 def finish(out_in, ig_in, sums_in, out_hbm, ig_hbm, wg_hbm, held, sums, share, in_sem, out_sem):
-    first = pltpu.make_async_copy(sums_in, sums, in_sem.at[8])
+    first = pltpu.make_async_copy(sums_in, sums, in_sem.at[2])
     first.start()
-    parts = [(i, slice(4 * n, 4 * n + 4)) for n in range(4) for i in range(2)]
+    parts = [(i, slice(0, LX)) for i in range(2)]
     loads = [
         pltpu.make_async_copy((out_in, ig_in)[i].at[x], held.at[i, x], in_sem.at[n]) for n, (i, x) in enumerate(parts)
     ]
@@ -420,7 +426,7 @@
     first.wait()
     share[0:HALF, :] = sums[0]
     share[HALF:SHARE, :] = sums[1, 0 : SHARE - HALF]
-    last = pltpu.make_async_copy(share, wg_hbm, out_sem.at[8])
+    last = pltpu.make_async_copy(share, wg_hbm, out_sem.at[2])
     last.start()
     for load, store in zip(loads, stores):
         load.wait()
@@ -495,8 +501,8 @@
             pltpu.VMEM((2,) + block, BF),
             pltpu.VMEM((2, HALF, C), F32),
             pltpu.VMEM((SHARE, C), F32),
-            dma((9,)),
-            dma((9,)),
+            dma((3,)),
+            dma((3,)),
         ],
         compiler_params=pltpu.CompilerParams(vmem_limit_bytes=60 * 1024 * 1024),
     )(output, input_grad, sums)

time: 36.2 us -> 36.2 us (level)
  no operation moved by 1% of the time
where the time goes in v5:
time: 36.2 us; the launch traced here: 36 us
  Pallas kernels  35.3 us (98%)
  between operations  0.64 us (2%)
    pallas_call x1, Pallas kernels, body(): pl.pallas_call(kernel, name='conv_and_grads', out_shape=(jax.ShapeDtypeSt...  33.3 us
    pallas_call x1, Pallas kernels, body(): pl.pallas_call(finish, name='write_results', out_shape=(jax.ShapeDtypeStr...  2.08 us

profile of v5, /device:TPU:1, one launch (start us, length us, event | category | flops | bytes accessed | tf_op | source)
XLA Modules:
  0.0 36.0 jit_solution(9815909987492429222)
XLA Ops:
  0.6 33.3 %conv_and_grads.1 = (bf16[16,16,8,128]{3,2,1,0:T(8,128)(2,1)}, bf16[16,16,8,128]{3,2,1,0:T(8,128)(2,1)}, f32[2,16,128]{2,1,0:T(8,128)}) custom-call(bf16[16,16,8,128]{3,2,1,0:T(8,128)(2,1)} %bitcast.9, bf16[16,16,8,128]{3,2,1,0:T(8,128)(2,1)} %bitcast.10, s32[18,10,1,18]{3,2,1,0:T(1,128)} %bitcast.11, s32[1,4]{1,0:T(1,128)} %bitcast.12, ...), custom_call_target="tpu_custom_call" | custom-call | tf_op jit(solution)/shard_map/conv_and_grads/pallas_call | solution.py:445
  33.9 2.1 %write_results.1 = (bf16[16,16,8,128]{3,2,1,0:T(8,128)(2,1)}, bf16[16,16,8,128]{3,2,1,0:T(8,128)(2,1)}, f32[27,128]{1,0:T(8,128)}) custom-call(bf16[16,16,8,128]{3,2,1,0:T(8,128)(2,1)} %get-tuple-element.9.out_in, bf16[16,16,8,128]{3,2,1,0:T(8,128)(2,1)} %get-tuple-element.10.ig_in, f32[2,16,128]{2,1,0:T(8,128)} %get-tuple-element.11.sums_in), custom_call_target="tpu_custom_call" | custom-call | tf_op jit(solution)/shard_map/write_results/pallas_call | solution.py:490
